TPU v7x, 256 devices: a whole 4x4x8 slice. The times are simulated.
256 devices in a mesh: graph: 64 (over x, z, core), feat: 4 (over y).
Axes of the slice: x: 4, y: 4, z: 8, core: 2. Of those that a mesh axis runs over, the one named last changes fastest.
Arguments:
- node_lat: bfloat16 [32768, 512], P(('graph', 'feat')), may hold values from -6 to 6
- coarse_lat: bfloat16 [256, 512], replicated, may hold values from -6 to 6
- edge_lat: bfloat16 [131072, 512], P(('graph', 'feat')), may hold values from -6 to 6
- senders: int32 [131072], P(('graph', 'feat')), may hold values from 0 to 1279, as said below
- receivers: int32 [131072], P(('graph', 'feat')), may hold values from 0 to 383, as said below
- halo_rows: int32 [16384, 8], P(('graph', 'feat')), may hold values from 0 to 511, as said below
- edge_live: int32 [256], P(('graph', 'feat')), may hold values from 128 to 512, as said below
- edge_first: bfloat16 [1536, 512], P('feat'), may hold values from -0.15625 to 0.15625
- edge_second: bfloat16 [512, 512], P('feat'), may hold values from -0.25 to 0.25
- node_first: bfloat16 [1024, 512], P('feat'), may hold values from -0.1875 to 0.1875
- node_second: bfloat16 [512, 512], P('feat'), may hold values from -0.25 to 0.25
- edge_gain: float32 [512], replicated, may hold values from 0.25 to 1.75
- node_gain: float32 [512], replicated, may hold values from 0.25 to 1.75
- node_cotangent: bfloat16 [32768, 512], P(('graph', 'feat')), may hold values from -6 to 6
- coarse_cotangent: bfloat16 [256, 512], replicated, may hold values from -6 to 6
- edge_cotangent: bfloat16 [131072, 512], P(('graph', 'feat')), may hold values from -6 to 6
Outputs:
- node_grad: float32 [32768, 512], P(('graph', 'feat'))
- coarse_grad: float32 [256, 512], replicated
- edge_grad: float32 [131072, 512], P(('graph', 'feat'))
- edge_first_grad: float32 [1536, 512], P('feat')
- edge_second_grad: float32 [512, 512], P('feat')
- node_first_grad: float32 [1024, 512], P('feat')
- node_second_grad: float32 [512, 512], P('feat')
Inputs may be any that keep to these rules, and one draw needn't show every extreme that they name: `senders`: codes as in the first step. `receivers`: codes as in the first step. `halo_rows`: rows within a part of 512 nodes. `edge_live`: some block is wholly live.
All inputs are finite; a program needn't handle non-finite values.
Results may differ from a plain program's by a relative error of at most 0.015.
Values may be sent and summed in bfloat16 or wider, within the bound.
A program may use at most 128 MiB of HBM per device.

v0:
```python
import jax
import jax.numpy as jnp
from jax import lax
from jax.sharding import PartitionSpec as P

NORM_EPSILON = 1e-05


def contract_rows(left, right):
    return lax.dot_general(
        left, right, (((0,), (0,)), ((), ())), preferred_element_type=jnp.float32
    )


def contract_last(left, right):
    return lax.dot_general(
        left, right, (((1,), (1,)), ((), ())), preferred_element_type=jnp.float32
    )


def mlp_forward(inputs, first, second):
    before = jnp.dot(inputs, first, preferred_element_type=jnp.float32)
    hidden = (before * jax.nn.sigmoid(before)).astype(jnp.bfloat16)
    output = jnp.dot(hidden, second, preferred_element_type=jnp.float32)
    centred = output - jnp.mean(output, axis=1, keepdims=True)
    inverse = lax.rsqrt(jnp.mean(centred * centred, axis=1, keepdims=True) + NORM_EPSILON)
    return (before, hidden, centred * inverse, inverse)


def mlp_backward(inputs, first, second, gain, saved, upstream, keeper):
    before, hidden, normed, inverse = saved
    scaled = upstream * gain
    grad_lin = inverse * (
        scaled
        - jnp.mean(scaled, axis=1, keepdims=True)
        - normed * jnp.mean(scaled * normed, axis=1, keepdims=True)
    )
    grad_lin = grad_lin.astype(jnp.bfloat16)
    grad_hidden = contract_last(grad_lin, second)
    sigma = jax.nn.sigmoid(before)
    grad_before = (grad_hidden * sigma * (1.0 + before * (1.0 - sigma))).astype(jnp.bfloat16)
    grad_inputs = contract_last(grad_before, first)
    if keeper is None:
        grad_second = contract_rows(hidden, grad_lin)
        grad_first = contract_rows(inputs, grad_before)
    else:
        grad_second = contract_rows(hidden, grad_lin * keeper)
        grad_first = contract_rows(inputs, grad_before * keeper)
    return (grad_inputs, grad_first, grad_second)


def node_pass(latents, aggregate, upstream_rows, first, second, gain, keeper):
    node_inputs = jnp.concatenate([latents, aggregate.astype(jnp.bfloat16)], axis=1)
    saved = mlp_forward(node_inputs, first, second)
    upstream = upstream_rows.astype(jnp.float32)
    grad_inputs, grad_first, grad_second = mlp_backward(
        node_inputs, first, second, gain, saved, upstream, keeper
    )
    latent_width = latents.shape[1]
    return (
        upstream + grad_inputs[:, :latent_width],
        grad_inputs[:, latent_width:],
        grad_first,
        grad_second,
    )


def body(
    node_lat,
    coarse_lat,
    edge_lat,
    senders,
    receivers,
    halo_rows,
    edge_live,
    edge_first,
    edge_second,
    node_first,
    node_second,
    edge_gain,
    node_gain,
    node_cotangent,
    coarse_cotangent,
    edge_cotangent,
):
    feat_count = lax.axis_size("feat")
    graph_count = lax.axis_size("graph")
    node_count = node_lat.shape[0]
    latent_width = node_lat.shape[1]
    coarse_count = coarse_lat.shape[0]
    edge_count = edge_lat.shape[0]
    part_rows = feat_count * node_count
    slot_rows = halo_rows.shape[0] * halo_rows.shape[1]
    feat_index = lax.axis_index("feat")
    device_index = lax.axis_index("graph") * feat_count + feat_index
    owned_rows = coarse_count // (graph_count * feat_count)
    part_nodes, first_edge, second_edge, first_node, second_node = (
        lax.all_gather(node_lat, "feat", axis=0, tiled=True),
        lax.all_gather(edge_first, "feat", axis=0, tiled=True),
        lax.all_gather(edge_second, "feat", axis=0, tiled=True),
        lax.all_gather(node_first, "feat", axis=0, tiled=True),
        lax.all_gather(node_second, "feat", axis=0, tiled=True),
    )
    outgoing = jnp.take(part_nodes, halo_rows.reshape(-1), axis=0)
    incoming = lax.all_to_all(outgoing, "graph", split_axis=0, concat_axis=0, tiled=True)
    node_table = jnp.concatenate([part_nodes, incoming, coarse_lat], axis=0)
    recv_index = jnp.where(
        receivers < node_count,
        feat_index * node_count + receivers,
        part_rows + slot_rows + receivers - node_count,
    )
    edge_inputs = jnp.concatenate(
        [edge_lat, jnp.take(node_table, senders, axis=0), jnp.take(node_table, recv_index, axis=0)],
        axis=1,
    )
    alive_mask = (lax.iota(jnp.int32, edge_count) < edge_live[0]).astype(jnp.float32)[:, None]
    edge_saved = mlp_forward(edge_inputs, first_edge, second_edge)
    edge_next = (edge_lat.astype(jnp.float32) + alive_mask * (edge_saved[2] * edge_gain)).astype(
        jnp.bfloat16
    )
    aggregate = jax.ops.segment_sum(
        alive_mask * edge_next.astype(jnp.float32),
        receivers,
        num_segments=node_count + coarse_count,
    )
    own_aggregate = aggregate[:node_count]
    coarse_aggregate = aggregate[node_count:]
    coarse_total = lax.psum(coarse_aggregate, ("graph", "feat"))
    row_index = lax.iota(jnp.int32, node_count + coarse_count) - node_count
    keeper = jnp.logical_or(row_index < 0, row_index // owned_rows == device_index).astype(
        jnp.bfloat16
    )[:, None]
    direct, grad_aggregate, node_first_term, node_second_term = node_pass(
        jnp.concatenate([node_lat, coarse_lat], axis=0),
        jnp.concatenate([own_aggregate, coarse_total], axis=0),
        jnp.concatenate([node_cotangent, coarse_cotangent], axis=0),
        first_node,
        second_node,
        node_gain,
        keeper,
    )
    grad_next = edge_cotangent.astype(jnp.float32) + alive_mask * jnp.take(
        grad_aggregate, receivers, axis=0
    )
    grad_inputs, edge_first_term, edge_second_term = mlp_backward(
        edge_inputs, first_edge, second_edge, edge_gain, edge_saved, alive_mask * grad_next, None
    )
    edge_grad = grad_next + grad_inputs[:, :latent_width]
    send_grads = jax.ops.segment_sum(
        grad_inputs[:, latent_width : 2 * latent_width],
        senders,
        num_segments=part_rows + slot_rows + coarse_count,
    )
    recv_grads = jax.ops.segment_sum(
        grad_inputs[:, 2 * latent_width :], receivers, num_segments=node_count + coarse_count
    )
    returned = lax.all_to_all(
        send_grads[part_rows : part_rows + slot_rows].astype(jnp.bfloat16),
        "graph",
        split_axis=0,
        concat_axis=0,
        tiled=True,
    ).astype(jnp.float32)
    part_grads = send_grads[:part_rows] + jax.ops.segment_sum(
        returned, halo_rows.reshape(-1), num_segments=part_rows
    )
    own_grads = lax.psum_scatter(
        part_grads.astype(jnp.bfloat16), "feat", scatter_dimension=0, tiled=True
    ).astype(jnp.float32)
    node_grad = direct[:node_count] + recv_grads[:node_count] + own_grads
    coarse_partial = send_grads[part_rows + slot_rows :] + recv_grads[node_count:]
    coarse_grad = direct[node_count:] + lax.psum(coarse_partial, ("graph", "feat"))
    grad_terms = (edge_first_term, edge_second_term, node_first_term, node_second_term)
    pieces = [
        grad_term.reshape(feat_count, grad_term.shape[0] // feat_count, latent_width)
        for grad_term in grad_terms
    ]
    stacked = jnp.concatenate(pieces, axis=1)
    slice_rows = stacked.shape[1]
    column_block = latent_width // graph_count
    arranged = (
        stacked.reshape(feat_count, slice_rows, graph_count, column_block)
        .transpose(1, 2, 0, 3)
        .reshape(slice_rows, latent_width * feat_count)
    )
    summed_piece = lax.psum_scatter(arranged, ("graph", "feat"), scatter_dimension=1, tiled=True)
    summed = lax.all_gather(summed_piece, "graph", axis=1, tiled=True)
    first_end = edge_first.shape[0]
    second_end = first_end + edge_second.shape[0]
    third_end = second_end + node_first.shape[0]
    return (
        node_grad,
        coarse_grad,
        edge_grad,
        summed[:first_end],
        summed[first_end:second_end],
        summed[second_end:third_end],
        summed[third_end:],
    )


def solution(mesh):
    return jax.shard_map(
        body,
        mesh=mesh,
        in_specs=(
            P(("graph", "feat"), None),
            P(),
            P(("graph", "feat"), None),
            P(("graph", "feat")),
            P(("graph", "feat")),
            P(("graph", "feat"), None),
            P(("graph", "feat")),
            P("feat", None),
            P("feat", None),
            P("feat", None),
            P("feat", None),
            P(),
            P(),
            P(("graph", "feat"), None),
            P(),
            P(("graph", "feat"), None),
        ),
        out_specs=(
            P(("graph", "feat"), None),
            P(),
            P(("graph", "feat"), None),
            P("feat", None),
            P("feat", None),
            P("feat", None),
            P("feat", None),
        ),
        check_vma=False,
    )
```

profile of v0, /device:TPU:1, one launch (start us, length us, event | category | flops | bytes accessed | tf_op | source)
XLA Modules:
  0.0 624.3 jit_solution(12355044645514905667)
XLA Ops:
  9.6 12.8 %all_gather.18 = bf16[512,512]{1,0:T(8,128)(2,1)S(1)} all-gather(bf16[128,512]{1,0:T(8,128)(2,1)} %param.18), channel_id=1, replica_groups=mesh['graph'=64,'feat'=4] {'feat'}, dimensions={0}, use_global_device_ids=true | all-gather | bytes 655360 | tf_op jit(solution)/shard_map/all_gather | solution.py:98
  25.4 13.7 %all-to-all-start = ((bf16[64,8,512]{2,1,0:T(8,128)(2,1)}), bf16[64,8,512]{2,1,0:T(8,128)(2,1)S(1)}, u32[]{:S(2)}, u32[]{:S(2)}) async-start(bf16[64,8,512]{2,1,0:T(8,128)(2,1)} %bitcast_select_fusion), calls=%async_computation | async-start | bytes 1048576 | tf_op jit(solution)/shard_map/all_to_all | solution.py:105
  41.9 12.0 %all_gather.20 = bf16[512,512]{1,0:T(8,128)(2,1)S(1)} all-gather(bf16[128,512]{1,0:T(8,128)(2,1)} %param.26), channel_id=1, replica_groups=mesh['graph'=64,'feat'=4] {'feat'}, dimensions={0}, use_global_device_ids=true | all-gather | bytes 655360 | tf_op jit(solution)/shard_map/all_gather | solution.py:100
  53.9 14.1 %all_gather.22 = bf16[512,512]{1,0:T(8,128)(2,1)} all-gather(bf16[128,512]{1,0:T(8,128)(2,1)} %param.28), channel_id=1, replica_groups=mesh['graph'=64,'feat'=4] {'feat'}, dimensions={0}, use_global_device_ids=true | all-gather | bytes 655360 | tf_op jit(solution)/shard_map/all_gather | solution.py:102
  71.8 2.6 gather_fusion.2
  75.8 3.8 multiply_convert_fusion.1
  82.4 4.5 scatter_custom_fusion
  87.8 82.8 %all-reduce.6 = bf16[256,512]{1,0:T(8,128)(2,1)S(1)} all-reduce(f32[256,512]{1,0:T(8,128)} %slice.83), channel_id=1, replica_groups=mesh['graph'=64,'feat'=4] {'graph','feat'}, use_global_device_ids=true, to_apply=%region_3.5 | all-reduce | flops 131072 | bytes 786432 | tf_op jit(solution)/shard_map/psum | solution.py:128
  176.3 2.2 fusion.25
  180.2 2.3 gather_fusion.1
  187.4 2.7 fusion.49
  190.1 5.2 scatter_custom_fusion.1
  195.3 5.9 scatter_custom_fusion.2
  201.2 4.3 fusion.19
  208.1 2.2 concatenate.39
  210.3 4.8 concatenate.37
  215.1 4.1 maximum_bitcast_fusion
  219.3 3.5 copy.60
  225.9 7.9 %all-to-all-start.1 = ((bf16[64,8,512]{2,1,0:T(8,128)(2,1)}), bf16[64,8,512]{2,1,0:T(8,128)(2,1)S(1)}, u32[]{:S(2)}, u32[]{:S(2)}) async-start(bf16[64,8,512]{2,1,0:T(8,128)(2,1)} %fusion.21), calls=%async_computation.1 | async-start | bytes 1048576 | tf_op jit(solution)/shard_map/all_to_all | solution.py:157
  234.0 19.6 %all-to-all-done.1 = bf16[64,8,512]{2,1,0:T(8,128)(2,1)S(1)} async-done(((bf16[64,8,512]{2,1,0:T(8,128)(2,1)}), bf16[64,8,512]{2,1,0:T(8,128)(2,1)S(1)}, u32[]{:S(2)}, u32[]{:S(2)}) %all-to-all-start.1) | async-done | bytes 524320 | tf_op jit(solution)/shard_map/all_to_all | solution.py:157
  253.6 4.1 scatter_custom_fusion.3
  258.6 246.2 %all-reduce.5.cloned.1.call-done = (f32[256,512]{1,0:T(8,128)}, f32[896,2048]{0,1:T(8,128)}) async-done(((f32[256,512]{1,0:T(8,128)}, f32[896,2048]{0,1:T(8,128)}), (f32[256,512]{1,0:T(8,128)}, f32[896,2048]{0,1:T(8,128)})) %all-reduce.5.cloned.1.call-update) | async-done | bytes 7864336 | tf_op jit(solution)/shard_map/psum | solution.py:172
  510.4 20.0 %reduce-scatter.2.cloned.1.call-done = bf16[128,512]{1,0:T(8,128)(2,1)} async-done(((bf16[512,512]{1,0:T(8,128)(2,1)}), bf16[128,512]{1,0:T(8,128)(2,1)}) %reduce-scatter.2.cloned.1.call-update) | async-done | bytes 131088 | tf_op jit(solution)/shard_map/reduce_scatter | solution.py:167
  533.0 79.8 %all-gather.8.cloned.1.call-done = f32[896,512]{0,1:T(8,128)} async-done(((f32[896,8]{0,1:T(8,128)}), f32[896,512]{0,1:T(8,128)}) %all-gather.8.cloned.1.call-update) | async-done | bytes 1835024 | tf_op jit(solution)/shard_map/all_gather | solution.py:187
  (153 shorter events, 48.3 us)
Async XLA Ops:
  7.2 68.6 %all-gather.4.cloned.1.call-start = ((), (), s32[]{:S(2)}) async-start(), calls=%async_computation.3 | async-start | bytes 1966080 | tf_op jit(solution)/shard_map/all_gather | solution.py:99
  24.4 16.2 %copy-start.30 = (s32[512]{0:T(512)S(1)}, s32[512]{0:T(512)}, u32[]{:S(2)}) copy-start(s32[512]{0:T(512)} %param.21) | copy-start | bytes 6148
  24.4 16.2 %copy-start.31 = (s32[512]{0:T(512)S(1)}, s32[512]{0:T(512)}, u32[]{:S(2)}) copy-start(s32[512]{0:T(512)} %param.22) | copy-start | bytes 6148
  24.4 16.2 %copy-start.18 = (bf16[512,512]{1,0:T(8,128)(2,1)S(1)}, bf16[512,512]{1,0:T(8,128)(2,1)}, u32[]{:S(2)}) copy-start(bf16[512,512]{1,0:T(8,128)(2,1)} %param.33) | copy-start | bytes 1572868
  24.4 16.4 %copy-start.19 = (bf16[512,512]{1,0:T(8,128)(2,1)S(1)}, bf16[512,512]{1,0:T(8,128)(2,1)}, u32[]{:S(2)}) copy-start(bf16[512,512]{1,0:T(8,128)(2,1)} %param.20) | copy-start | bytes 1572868
  25.4 42.6 %all-to-all-start = ((bf16[64,8,512]{2,1,0:T(8,128)(2,1)}), bf16[64,8,512]{2,1,0:T(8,128)(2,1)S(1)}, u32[]{:S(2)}, u32[]{:S(2)}) async-start(bf16[64,8,512]{2,1,0:T(8,128)(2,1)} %bitcast_select_fusion), calls=%async_computation | async-start | bytes 1048576 | tf_op jit(solution)/shard_map/all_to_all | solution.py:105
  39.0 29.7 %copy-start.23 = (bf16[256,512]{1,0:T(8,128)(2,1)S(1)}, bf16[256,512]{1,0:T(8,128)(2,1)}, u32[]{:S(2)}) copy-start(bf16[256,512]{1,0:T(8,128)(2,1)} %param.19) | copy-start | bytes 786436
  39.1 131.6 %all-gather.6.cloned.1.call-start = ((), (), s32[]{:S(2)}) async-start(), calls=%async_computation.4 | async-start | bytes 1310720 | tf_op jit(solution)/shard_map/all_gather | solution.py:101
  39.8 465.0 %all-reduce.5.cloned.1.call-start = ((), (), s32[]{:S(2)}) async-start(), calls=%async_computation.7 | async-start | bytes 15728640 | tf_op jit(solution)/shard_map/psum | solution.py:172
  40.8 143.7 %copy-start.1 = (bf16[512,512]{0,1:T(8,128)(2,1)}, bf16[512,512]{0,1:T(8,128)(2,1)S(1)}, u32[]{:S(2)}) copy-start(bf16[512,512]{0,1:T(8,128)(2,1)S(1)} %copy.52) | copy-start | bytes 1572868
  75.8 3.8 copy-start.21
  75.8 3.8 copy-start.22
  82.4 88.2 %copy-start.24 = (bf16[128,512]{1,0:T(8,128)(2,1)S(1)}, bf16[128,512]{1,0:T(8,128)(2,1)}, u32[]{:S(2)}) copy-start(bf16[128,512]{1,0:T(8,128)(2,1)} %param.18) | copy-start | bytes 393220
  86.9 83.7 %copy-start.26 = (bf16[128,512]{1,0:T(8,128)(2,1)}, bf16[128,512]{1,0:T(8,128)(2,1)S(1)}, u32[]{:S(2)}) copy-start(bf16[128,512]{1,0:T(8,128)(2,1)S(1)} %slice.116) | copy-start | bytes 393220
  201.2 4.3 copy-start.14
  219.3 3.6 copy-start
  219.3 3.6 copy-start.4
  223.7 29.9 %slice-start.1 = ((f32[1280,512]{1,0:T(8,128)}), f32[512,512]{1,0:T(8,128)S(1)}, s32[]{:S(2)}) async-start(f32[1280,512]{1,0:T(8,128)} %scatter_custom_fusion.2), calls=%async_computation.9 | async-start | bytes 2097152 | tf_op jit(solution)/shard_map/slice | solution.py:164
  225.9 27.7 %all-to-all-start.1 = ((bf16[64,8,512]{2,1,0:T(8,128)(2,1)}), bf16[64,8,512]{2,1,0:T(8,128)(2,1)S(1)}, u32[]{:S(2)}, u32[]{:S(2)}) async-start(bf16[64,8,512]{2,1,0:T(8,128)(2,1)} %fusion.21), calls=%async_computation.1 | async-start | bytes 1048576 | tf_op jit(solution)/shard_map/all_to_all | solution.py:157
  233.8 296.6 %reduce-scatter.2.cloned.1.call-start = ((), (), s32[]{:S(2)}) async-start(), calls=%async_computation.5 | async-start | bytes 655360 | tf_op jit(solution)/shard_map/reduce_scatter | solution.py:167
  257.7 248.5 %slice-start = ((f32[512,1536]{1,0:T(8,128)}), f32[512,512]{1,0:T(8,128)S(1)}, s32[]{:S(2)}) async-start(f32[512,1536]{1,0:T(8,128)} %fusion.49), calls=%async_computation.8 | async-start | bytes 2097152 | tf_op jit(solution)/shard_map/slice | solution.py:148
  258.6 354.2 %all-gather.8.cloned.1.call-start = ((), (), s32[]{:S(2)}) async-start(), calls=%async_computation.6 | async-start | bytes 1863680 | tf_op jit(solution)/shard_map/all_gather | solution.py:187
  507.5 22.9 %copy-start.3 = (f32[384,512]{1,0:T(8,128)S(1)}, f32[384,512]{1,0:T(8,128)}, u32[]{:S(2)}) copy-start(f32[384,512]{1,0:T(8,128)} %get-tuple-element.39) | copy-start | bytes 2359300
  509.1 23.0 %copy-start.15 = (f32[256,512]{1,0:T(8,128)S(1)}, f32[256,512]{1,0:T(8,128)}, u32[]{:S(2)}) copy-start(f32[256,512]{1,0:T(8,128)} %get-tuple-element.33) | copy-start | bytes 1572868
  (19 other events, 27.9 us)
Sparse Core Ops, SparseCore 0:
  9.8 32.8 all-gather.3
  44.6 28.2 all-gather.5
  223.8 280.9 all-reduce.4
  507.9 22.4 reduce-scatter.1
  533.9 78.8 all-gather.7
where the time goes:
time: 626 us; the launch traced here: 624 us
  waiting for transfers between devices  367 us (59%)
  blocking collectives  122 us (19%)
  local copies, waits for them, and re-layouts  42.2 us (7%)
  other arithmetic  37.1 us (6%)
  starting transfers between devices  21.8 us (3%)
  matrix products  19.5 us (3%)
  between operations  15.1 us (2%)
    psum x1, waiting for transfers between devices, body(): lax.psum(coarse_partial, ('graph', 'feat'))  246 us
    psum x1, blocking collectives, body(): coarse_total = lax.psum(coarse_aggregate, ('graph', 'feat'))  82.8 us
    all_gather x1, waiting for transfers between devices, body(): summed = lax.all_gather(summed_piece, 'graph', axis=1, tiled=True)  79.8 us
    reduce_scatter x1, waiting for transfers between devices, body(): lax.psum_scatter(part_grads.astype(jnp.bfloat16), 'feat', scatter_dimensi...  20 us
    all_to_all x1, waiting for transfers between devices, body(): lax.all_to_all(send_grads[part_rows:part_rows + slot_rows].astype(jnp.bfl...  19.6 us
    all_gather x1, blocking collectives, body(): lax.all_gather(node_second, 'feat', axis=0, tiled=True)  14.1 us
    all_to_all x1, starting transfers between devices, body(): lax.all_to_all(outgoing, 'graph', split_axis=0, concat_axis=0, tiled=True)  13.7 us
    all_gather x1, blocking collectives, body(): lax.all_gather(node_lat, 'feat', axis=0, tiled=True)  12.8 us
  transfers between devices with their start and end apart: 7, of which 4 were waited for; matrix products, arithmetic and copies ran while one was open for 6% of the time, Pallas kernels for 0%

commit v1 on v0

v1 whole, which is shorter than its diff:
```python
import functools

import jax
import jax.numpy as jnp
from jax import lax
from jax.experimental import pallas as pl
from jax.experimental.pallas import tpu as pltpu
from jax.sharding import PartitionSpec as P

NORM_EPSILON = 1e-05
F32 = jnp.float32
BF16 = jnp.bfloat16
MESH = pl.DeviceIdType.MESH

D = 512
N = 128
E = 512
C = 256
NX, NY, NZ, NC = 4, 4, 8, 2
G = NX * NZ * NC
HALO = 8
RE, RN = 256, 192
ZR = 32
PLANE = NX * NZ


def dot(a, b):
    return jnp.dot(a, b, preferred_element_type=F32)


def dot_nt(a, b):
    return lax.dot_general(a, b, (((1,), (1,)), ((), ())), preferred_element_type=F32)


def dot_tn(a, b):
    return lax.dot_general(a, b, (((0,), (0,)), ((), ())), preferred_element_type=F32)


def xor4(v, j):
    return (v, v + 1 - 2 * (v % 2), (v + 2) % 4, 3 - v)[j]


def aligned(index, by):
    return pl.multiple_of(index, by)


def normalise(output):
    centred = output - jnp.mean(output, axis=1, keepdims=True)
    inverse = lax.rsqrt(jnp.mean(centred * centred, axis=1, keepdims=True) + NORM_EPSILON)
    return centred * inverse, inverse


def norm_backward(upstream, gain, normed, inverse):
    scaled = upstream * gain
    grad = inverse * (
        scaled
        - jnp.mean(scaled, axis=1, keepdims=True)
        - normed * jnp.mean(scaled * normed, axis=1, keepdims=True)
    )
    return grad.astype(BF16)


def silu_backward(grad_hidden, before):
    sigma = jax.nn.sigmoid(before)
    return (grad_hidden * sigma * (1.0 + before * (1.0 - sigma))).astype(BF16)


SCRATCH = dict(
    nodes=((NY, N, D), BF16),
    ef=((3 * D, D), BF16),
    es=((D, D), BF16),
    nf=((2 * D, D), BF16),
    ns=((D, D), BF16),
    halo_hot=((G * HALO, NY * N), BF16),
    halo_hot_t=((NY * N, G * HALO), BF16),
    send_hot=((E, 1280), BF16),
    send_hot_t=((1280, E), BF16),
    recv_hot=((E, N + C), BF16),
    recv_hot_t=((N + C, E), BF16),
    out_slots=((G, 16, 256), BF16),
    in_slots=((G, 16, 256), BF16),
    back_out=((G, 16, 256), BF16),
    back_in=((G, 16, 256), BF16),
    halo=((G * HALO, D), BF16),
    edge_in=((E, 3 * D), BF16),
    before=((E, D), F32),
    hidden=((E, D), BF16),
    normed=((E, D), F32),
    inverse=((E, 1), F32),
    lin=((E, D), BF16),
    gbefore=((E, D), BF16),
    gnext=((E, D), F32),
    moved=((E, D), BF16),
    node_in=((N + C, 2 * D), BF16),
    n_before=((N + C, D), F32),
    n_hidden=((N + C, D), BF16),
    n_normed=((N + C, D), F32),
    n_inverse=((N + C, 1), F32),
    n_lin=((N + C, D), BF16),
    n_gbefore=((N + C, D), BF16),
    direct=((N + C, D), F32),
    gagg=((N + C, D), BF16),
    coarse_total=((C, D), BF16),
    coarse_part=((C, D), F32),
    recv_own=((N, D), F32),
    part_grads=((NY * N, D), F32),
    a1_src=((32, 16, 256), BF16),
    a1_rs=((32, 16, 256), BF16),
    a1_z=((NZ, 16, 256), BF16),
    a1_ag=((32, 16, 256), BF16),
    a2_src=((32, 16, 256), BF16),
    a2_rs=((32, 16, 256), BF16),
    a2_z=((NZ, 16, 256), BF16),
    a2_ag=((32, 16, 256), BF16),
    v_node_cot=((N, D), BF16),
    v_coarse_cot=((C, D), BF16),
    v_edge_cot=((E, D), BF16),
    v_edge_grad=((E, D), F32),
    v_node_grad=((N, D), F32),
    v_coarse_grad=((C, D), F32),
    p_y=((NY, N, D), BF16),
    p_a1=((2, N // 2, D), BF16),
    p_b1=((2, N // 2, D), BF16),
    p_a2=((N // 2, D), BF16),
    p_b2=((N // 2, D), BF16),
)


def job_scratch(r):
    return dict(
        w=((NY, 2 * r, D), BF16),
        c=((NY, r, D), BF16),
        y=((NY, r, D), BF16),
        ya1=((2, r // 2, D), BF16),
        yb1=((2, r // 2, D), BF16),
        ya2=((r // 2, D), BF16),
        yb2=((r // 2, D), BF16),
        sum=((r, D), F32),
    )


EDGE_JOB, NODE_JOB = job_scratch(RE), job_scratch(RN)
EDGE_JOB.update(
    ps=((PLANE, 16, 256), BF16),
    pr=((PLANE, 16, 256), BF16),
    g=((PLANE, 16, 256), BF16),
)
NODE_JOB.update(
    x=((NX, RN, 128), BF16),
    xa1=((2, RN // 2, 128), BF16),
    xb1=((2, RN // 2, 128), BF16),
    xa2=((RN // 2, 128), BF16),
    xb2=((RN // 2, 128), BF16),
    zs=((NZ, ZR, 128), BF16),
    zr=((NZ, ZR, 128), BF16),
    g=((NX, NZ, ZR, 128), BF16),
    extra=((NC, NZ * ZR, D), F32),
)
SENDS, LOCALS = 76, 16

SMALL, LARGE = True, False
INPUTS = dict(
    node_lat=LARGE, coarse_lat=LARGE, edge_lat=LARGE, senders=SMALL, receivers=SMALL, halo_rows=SMALL,
    edge_live=SMALL, w_ef=LARGE, w_es=LARGE, w_nf=LARGE, w_ns=LARGE, edge_gain=SMALL, node_gain=SMALL,
    node_cot=LARGE, coarse_cot=LARGE, edge_cot=LARGE,
)
OUTPUTS = dict(
    node_grad=((N, D), F32),
    coarse_grad=((C, D), F32),
    edge_grad=((E, D), F32),
    e_grad=((NC, PLANE, 16, 256), BF16),
    n_grad=((NC, NX, NZ, ZR, 128), BF16),
)


class Refs(dict):
    __getattr__ = dict.__getitem__


class Links:
    def __init__(self, send_sems, recv_sems, local_sems):
        self.send_sems, self.recv_sems, self.used, self.sent = send_sems, recv_sems, 0, []
        self.local_sems, self.local_used = local_sems, 0
        graph = lax.axis_index("graph")
        self.g, self.y = graph, lax.axis_index("feat")
        self.c, self.z, self.x = graph % 2, (graph // 2) % 8, graph // 16

    def slot(self):
        self.used += 1
        return self.used - 1

    def at(self, x=None, y=None, z=None, c=None):
        x = self.x if x is None else x
        y = self.y if y is None else y
        z = self.z if z is None else z
        c = self.c if c is None else c
        return ((x * 8 + z) * 2 + c, y)

    def local(self, src, dst):
        copy = pltpu.make_async_copy(src, dst, self.local_sems.at[self.local_used])
        self.local_used += 1
        copy.start()
        return copy

    def send(self, src, dst, device):
        k = self.slot()
        copy = pltpu.make_async_remote_copy(
            src_ref=src,
            dst_ref=dst,
            send_sem=self.send_sems.at[k],
            recv_sem=self.recv_sems.at[k],
            device_id=device,
            device_id_type=MESH,
        )
        copy.start()
        self.sent.append(copy)
        return copy

    def send_many(self, count, peer, src, dst, whole):
        k = self.slot()

        def body(j, carry):
            index, device = peer(j)
            pltpu.make_async_remote_copy(
                src_ref=src(index),
                dst_ref=dst,
                send_sem=self.send_sems.at[k],
                recv_sem=self.recv_sems.at[k],
                device_id=device,
                device_id_type=MESH,
            ).start()
            return carry

        lax.fori_loop(1, count, body, 0)
        self.sent.append(("many", whole, k))

        def wait():
            pltpu.make_async_copy(whole, whole, self.recv_sems.at[k]).wait()

        return wait

    def finish(self):
        for copy in self.sent:
            if isinstance(copy, tuple):
                pltpu.make_async_copy(copy[1], copy[1], self.send_sems.at[copy[2]]).wait()
            else:
                copy.wait_send()


def to_slots(rows):
    rows = rows.reshape(G, HALO, D)
    return jnp.concatenate([rows[:, :, :256], rows[:, :, 256:]], axis=1).astype(BF16)


def from_slots(slots):
    slots = slots.astype(F32)
    rows = jnp.concatenate([slots[:, :8, :], slots[:, 8:, :]], axis=2)
    return rows.reshape(G * HALO, D).astype(BF16)


def halving(links, buf, half, ra1, rb1, ra2, rb2, partner, total_out):
    lo, hi = pl.ds(0, half), pl.ds(half, half)
    p1, p3 = partner(1), partner(3)
    a = links.send(buf.at[pl.ds(1, 2), lo], ra1, p1)
    b = links.send(buf.at[pl.ds(2, 2), hi], rb1, p3)
    yield
    a.wait_recv()
    buf[3, lo] = (buf[3, lo].astype(F32) + ra1[1].astype(F32)).astype(BF16)
    a = links.send(buf.at[3, lo], ra2, p3)
    b.wait_recv()
    buf[1, hi] = (buf[1, hi].astype(F32) + rb1[0].astype(F32)).astype(BF16)
    b = links.send(buf.at[1, hi], rb2, p1)
    total_out[lo] = buf[0, lo].astype(F32) + ra1[0].astype(F32)
    total_out[hi] = buf[0, hi].astype(F32) + rb1[1].astype(F32)
    yield
    a.wait_recv()
    total_out[lo] = total_out[lo] + ra2[...].astype(F32)
    b.wait_recv()
    total_out[hi] = total_out[hi] + rb2[...].astype(F32)


def coarse_sum(links, source, src, rs, zb, ag, out):
    me = (links.x * 4 + links.y) * 2 + links.c

    def peer(j):
        m = (me + j * 11) % 32
        return m, links.at(x=m // 8, y=(m // 2) % 4, c=m % 2)

    for i in range(32):
        src[i] = source[(i // 2) * 16 : (i // 2) * 16 + 16, (i % 2) * 256 : (i % 2) * 256 + 256].astype(BF16)
    wait = links.send_many(32, peer, lambda m: src.at[m], rs.at[me], rs.at[pl.ds(0, 31)])
    rs[me] = src[me]
    yield
    wait()
    zb[links.z] = jnp.sum(rs[...].astype(F32), axis=0).astype(BF16)

    def along(j):
        to = (links.z + j * 3) % 8
        return to, links.at(z=to)

    wait = links.send_many(8, along, lambda m: zb.at[links.z], zb.at[links.z], zb.at[pl.ds(0, 7)])
    yield
    wait()
    ag[me] = jnp.sum(zb[...].astype(F32), axis=0).astype(BF16)
    wait = links.send_many(32, peer, lambda m: ag.at[me], ag.at[me], ag.at[pl.ds(0, 31)])
    yield
    wait()
    for i in range(32):
        out[(i // 2) * 16 : (i // 2) * 16 + 16, (i % 2) * 256 : (i % 2) * 256 + 256] = ag[i].astype(out.dtype)


def weight_scatter(links, t, r, fill):
    w, cin, ybuf = t.w, t.c, t.y
    other = links.at(c=1 - links.c)
    theirs = pl.ds(aligned((1 - links.c) * r, 16), r)
    mine = pl.ds(aligned(links.c * r, 16), r)
    copies = {}
    for j in (2, 1, 3, 0):
        fill(j, xor4(links.y, j))
        copies[j] = links.send(w.at[j, theirs], cin.at[j], other)
    yield
    for j in (2, 1, 3, 0):
        copies[j].wait_recv()
        ybuf[j] = (w[j, mine].astype(F32) + cin[j].astype(F32)).astype(BF16)
    total = t.sum
    yield from halving(
        links, ybuf, r // 2, t.ya1, t.yb1, t.ya2, t.yb2,
        lambda j: links.at(y=xor4(links.y, j)), total,
    )


def edge_weights_sum(links, t, r, fill, out):
    yield from weight_scatter(links, t, r, fill)
    total, ps, pr, gathered = t.sum, t.ps, t.pr, t.g
    for i in range(PLANE):
        ps[i] = total[(i // 2) * 16 : (i // 2) * 16 + 16, (i % 2) * 256 : (i % 2) * 256 + 256].astype(BF16)
    me = links.x * NZ + links.z

    def peer(k):
        m = (me + k * 11) % PLANE
        return m, links.at(x=m // NZ, z=m % NZ)

    wait = links.send_many(PLANE, peer, lambda m: ps.at[m], pr.at[me], pr.at[pl.ds(0, PLANE - 1)])
    pr[me] = ps[me]
    yield
    wait()
    gathered[me] = jnp.sum(pr[...].astype(F32), axis=0).astype(BF16)
    wait = links.send_many(
        PLANE, peer, lambda m: gathered.at[me], gathered.at[me], gathered.at[pl.ds(0, PLANE - 1)]
    )
    yield
    wait()
    copy = links.send(gathered, out.at[links.c], links.at(c=1 - links.c))
    own = links.local(gathered, out.at[links.c])
    yield
    copy.wait_recv()
    own.wait()


def node_weights_sum(links, t, r, fill, out):
    yield from weight_scatter(links, t, r, fill)
    for j in range(4):
        t.x[j] = t.sum[:, pl.ds(aligned(xor4(links.x, j) * 128, 128), 128)].astype(BF16)
    sub = t.sum.at[:, pl.ds(0, 128)]
    yield from halving(
        links, t.x, r // 2, t.xa1, t.xb1, t.xa2, t.xb2, lambda j: links.at(x=xor4(links.x, j)), sub
    )
    blocks = r // ZR
    for i in range(NZ):
        t.zs[i] = sub[i * ZR : (i + 1) * ZR].astype(BF16) if i < blocks else jnp.zeros((ZR, 128), BF16)

    def along(j):
        to = (links.z + j * 3) % NZ
        return to, links.at(z=to)

    wait = links.send_many(NZ, along, lambda m: t.zs.at[m], t.zr.at[links.z], t.zr.at[pl.ds(0, NZ - 1)])
    t.zr[links.z] = t.zs[links.z]
    yield
    wait()
    own = t.g.at[links.x]
    extra = t.extra[
        links.c, pl.ds(aligned(links.z * ZR, ZR), ZR), pl.ds(aligned(links.x * 128, 128), 128)
    ]
    own[links.z] = (jnp.sum(t.zr[...].astype(F32), axis=0) + extra).astype(BF16)
    wait = links.send_many(NZ, along, lambda m: own.at[links.z], own.at[links.z], own.at[pl.ds(0, NZ - 1)])
    yield
    wait()
    x1, x2, x3 = xor4(links.x, 1), xor4(links.x, 2), xor4(links.x, 3)
    every, lo, hi = pl.ds(0, blocks), pl.ds(0, blocks // 2), pl.ds(blocks // 2, blocks // 2)
    mine = t.g.at[links.x, every]
    a = links.send(mine, mine, links.at(x=x1))
    b = links.send(mine, mine, links.at(x=x3))
    yield
    a.wait_recv()
    a = links.send(t.g.at[x1, lo], t.g.at[x1, lo], links.at(x=x3))
    b.wait_recv()
    b = links.send(t.g.at[x3, hi], t.g.at[x3, hi], links.at(x=x1))
    yield
    a.wait_recv()
    b.wait_recv()
    result = t.g.at[:, every]
    copy = links.send(result, out.at[links.c, :, every], links.at(c=1 - links.c))
    local = links.local(result, out.at[links.c, :, every])
    yield
    copy.wait_recv()
    local.wait()


def body(*refs):
    refs = iter(refs)
    s = Refs(zip([*INPUTS, *OUTPUTS, *SCRATCH], refs))
    edge_refs, node_refs = Refs(zip(EDGE_JOB, refs)), Refs(zip(NODE_JOB, refs))
    links = Links(*refs)
    x, y, z, c, g = links.x, links.y, links.z, links.c, links.g
    y1, y2, y3 = xor4(y, 1), xor4(y, 2), xor4(y, 3)
    other = links.at(c=1 - c)
    ef, es, nf, ns = s.ef, s.es, s.nf, s.ns
    weights = {"ef": 384, "es": 128, "nf": 256, "ns": 128}
    nodes, edge_in, node_in = s.nodes, s.edge_in, s.node_in

    barrier = pltpu.get_barrier_semaphore()

    def greet_graph(j, carry):
        pl.semaphore_signal(barrier, inc=1, device_id=((g + j) % G, y), device_id_type=MESH)
        return carry

    def greet_plane(j, carry):
        k = j // 3
        device = links.at(x=k // 2, c=k % 2, y=(y + 1 + j % 3) % 4)
        pl.semaphore_signal(barrier, inc=1, device_id=device, device_id_type=MESH)
        return carry

    lax.fori_loop(1, G, greet_graph, 0)
    lax.fori_loop(0, 24, greet_plane, 0)
    early = [
        links.local(s.node_lat, nodes.at[y]),
        links.local(s.node_lat, node_in.at[pl.ds(0, N), pl.ds(0, D)]),
        links.local(s.coarse_lat, node_in.at[pl.ds(N, C), pl.ds(0, D)]),
        links.local(s.edge_lat, edge_in.at[:, pl.ds(0, D)]),
    ]
    for name, rows in weights.items():
        early.append(links.local(s["w_" + name], s[name].at[pl.ds(aligned(y * rows, 16), rows)]))
    for name in ("node_cot", "coarse_cot", "edge_cot"):
        early.append(links.local(s[name], s["v_" + name]))
    pl.semaphore_wait(barrier, G - 1 + 24)

    lo, hi = pl.ds(0, N // 2), pl.ds(N // 2, N // 2)
    lat = s.node_lat
    a_lo = links.send(lat.at[lo], nodes.at[y, lo], links.at(y=y1))
    b_hi = links.send(lat.at[hi], nodes.at[y, hi], links.at(y=y3))
    a_hi = links.send(lat.at[hi], nodes.at[y, hi], links.at(y=y1))
    b_lo = links.send(lat.at[lo], nodes.at[y, lo], links.at(y=y3))

    lanes = lax.broadcasted_iota(jnp.int32, (E, 128), 1)
    subs = lax.broadcasted_iota(jnp.int32, (128, E), 0)

    def hot(code_row, hot_ref, hot_t_ref, width):
        across = jnp.broadcast_to(code_row, (128, E))
        down = jnp.transpose(across)
        for j in range(width // 128):
            hot_ref[:, j * 128 : (j + 1) * 128] = jnp.where(down == lanes + j * 128, 1.0, 0.0).astype(BF16)
            hot_t_ref[j * 128 : (j + 1) * 128, :] = jnp.where(across == subs + j * 128, 1.0, 0.0).astype(BF16)

    codes = s.halo_rows[...]
    spread = (
        lax.broadcasted_iota(jnp.int32, (G, G * HALO), 0)
        == lax.broadcasted_iota(jnp.int32, (G, G * HALO), 1) // HALO
    )
    spread = jnp.where(spread, 1.0, 0.0).astype(BF16)
    high = dot((codes // 16).astype(F32).astype(BF16), spread)
    low = dot((codes % 16).astype(F32).astype(BF16), spread)
    shape = (HALO, G * HALO)
    at_k = lax.broadcasted_iota(jnp.int32, shape, 0) == lax.broadcasted_iota(jnp.int32, shape, 1) % HALO
    codes = jnp.sum(jnp.where(at_k, high * 16.0 + low, 0.0), axis=0, keepdims=True).astype(jnp.int32)
    hot(codes, s.halo_hot, s.halo_hot_t, NY * N)
    for copy in early:
        copy.wait()

    a_lo.wait_recv()
    a2 = links.send(nodes.at[y1, lo], nodes.at[y1, lo], links.at(y=y3))
    b_hi.wait_recv()
    b2 = links.send(nodes.at[y3, hi], nodes.at[y3, hi], links.at(y=y1))

    def weight_rows(name, owner, first, count):
        rows = weights[name]
        return s[name].at[pl.ds(aligned(owner * rows + c * (rows // 2) + first, 16), count)]

    def weight_step1(group):
        copies = []
        for name in group:
            half = weights[name] // 2
            src = s["w_" + name].at[pl.ds(aligned(c * half, 16), half)]
            copies.append(
                (
                    name,
                    links.send(src, weight_rows(name, y, 0, half), links.at(y=y1)),
                    links.send(src, weight_rows(name, y, 0, half), links.at(y=y3)),
                )
            )
        return copies

    def weight_step2(copies):
        forward, swap = [], []
        for name, first, second in copies:
            half, quarter = weights[name] // 2, weights[name] // 4
            first.wait_recv()
            src = weight_rows(name, y1, 0, quarter)
            forward.append(links.send(src, src, links.at(y=y3)))
            src = weight_rows(name, y1, 0, half)
            swap.append(links.send(src, src, other))
            second.wait_recv()
            src = weight_rows(name, y3, quarter, quarter)
            forward.append(links.send(src, src, links.at(y=y1)))
            src = weight_rows(name, y3, 0, half)
            swap.append(links.send(src, src, other))
        return forward, swap

    def weight_step3(group, forward, swap):
        for copy in forward:
            copy.wait_recv()
        for name in group:
            src = weight_rows(name, y2, 0, weights[name] // 2)
            swap.append(links.send(src, src, other))
        return swap

    for copy in (a_hi, b_lo, a2, b2):
        copy.wait_recv()
    edge_weights = weight_step1(("ef", "es"))

    out_slots, in_slots = s.out_slots, s.in_slots
    part_nodes = nodes[...].reshape(NY * N, D)
    out_slots[...] = to_slots(dot(s.halo_hot[...], part_nodes))

    def graph_peer(j):
        to = (g + j * 29) % G
        return to, (to, y)

    halo_wait = links.send_many(
        G, graph_peer, lambda m: out_slots.at[m], in_slots.at[g], in_slots.at[pl.ds(0, G - 1)]
    )
    in_slots[g] = out_slots[g]

    live = s.edge_live[...]
    alive_row = lax.broadcasted_iota(jnp.int32, (1, E), 1) < live
    hot(jnp.where(alive_row, s.senders[...], -1), s.send_hot, s.send_hot_t, 1280)
    hot(jnp.where(alive_row, s.receivers[...], -1), s.recv_hot, s.recv_hot_t, N + C)
    node_lat, coarse_lat = node_in[:N, :D], node_in[N:, :D]
    edge_in[:, 2 * D :] = (
        dot(s.recv_hot[:, :N], node_lat) + dot(s.recv_hot[:, N:], coarse_lat)
    ).astype(BF16)
    edge_in[:, D : 2 * D] = (
        dot(s.send_hot[:, :512], part_nodes) + dot(s.send_hot[:, 1024:], coarse_lat)
    ).astype(BF16)
    edge_forward, edge_swap = weight_step2(edge_weights)
    node_weights = weight_step1(("nf", "ns"))
    edge_swap = weight_step3(("ef", "es"), edge_forward, edge_swap)
    for copy in edge_swap:
        copy.wait_recv()
    before = s.before
    before[...] = dot(edge_in[:, :D], ef[:D]) + dot(edge_in[:, 2 * D :], ef[2 * D :])

    node_forward, node_swap = weight_step2(node_weights)

    halo_wait()
    s.halo[...] = from_slots(in_slots[...])
    edge_in[:, D : 2 * D] = (
        edge_in[:, D : 2 * D].astype(F32) + dot(s.send_hot[:, 512:1024], s.halo[...])
    ).astype(BF16)
    before[...] = before[...] + dot(edge_in[:, D : 2 * D], ef[D : 2 * D])
    s.hidden[...] = (before[...] * jax.nn.sigmoid(before[...])).astype(BF16)
    normed, inverse = normalise(dot(s.hidden[...], es[...]))
    s.normed[...] = normed
    s.inverse[...] = inverse
    edge_next = (edge_in[:, :D].astype(F32) + normed * s.edge_gain[...]).astype(BF16)
    s.coarse_part[...] = dot(s.recv_hot_t[N:], edge_next)
    total = coarse_sum(
        links, s.coarse_part, s.a1_src, s.a1_rs, s.a1_z, s.a1_ag, s.coarse_total
    )
    next(total)
    own_agg = dot(s.recv_hot_t[:N], edge_next).astype(BF16)
    node_in[:N, D:] = own_agg
    node_swap = weight_step3(("nf", "ns"), node_forward, node_swap)

    def node_up(rows):
        name = "v_node_cot" if rows.start == 0 else "v_coarse_cot"
        return s[name][...].astype(F32)

    def node_pass_forward(rows):
        a = dot(node_in[rows], nf[...])
        hidden = (a * jax.nn.sigmoid(a)).astype(BF16)
        s.n_before[rows] = a
        s.n_hidden[rows] = hidden
        n, inv = normalise(dot(hidden, ns[...]))
        s.n_normed[rows] = n
        s.n_inverse[rows] = inv

    def node_pass_backward(rows):
        up = node_up(rows)
        q = norm_backward(up, s.node_gain[...], s.n_normed[rows], s.n_inverse[rows])
        zz = silu_backward(dot_nt(q, ns[...]), s.n_before[rows])
        s.n_lin[rows] = q
        s.n_gbefore[rows] = zz
        s.direct[rows] = up + dot_nt(zz, nf[:D])
        s.gagg[rows] = dot_nt(zz, nf[D:]).astype(BF16)

    own, coarse = slice(0, N), slice(N, N + C)

    def fill_node(j, to):
        w = node_refs.w
        w[j, :256] = dot_tn(node_in[:N, pl.ds(aligned(to * 256, 128), 256)], s.n_gbefore[:N]).astype(BF16)
        w[j, 256:] = dot_tn(s.n_hidden[:N, pl.ds(aligned(to * 128, 128), 128)], s.n_lin[:N]).astype(BF16)

    node_job = node_weights_sum(links, node_refs, RN, fill_node, s.n_grad)
    next(total)
    for copy in node_swap:
        copy.wait_recv()
    node_pass_forward(own)
    node_pass_backward(own)
    next(node_job)
    next(total)
    next(node_job)
    for _ in total:
        pass
    node_in[N:, D:] = s.coarse_total[...]
    node_pass_forward(coarse)
    node_pass_backward(coarse)

    s.gnext[...] = s.v_edge_cot[...].astype(F32) + dot(s.recv_hot[...], s.gagg[...])
    alive = lax.broadcasted_iota(jnp.int32, (E, 1), 0) < live
    upstream = jnp.where(alive, s.gnext[...], 0.0)
    q = norm_backward(upstream, s.edge_gain[...], s.normed[...], s.inverse[...])
    s.lin[...] = q
    s.gbefore[...] = silu_backward(dot_nt(q, es[...]), before[...])
    gbefore = s.gbefore

    def fill_edge(j, to):
        w = edge_refs.w
        w[j, :384] = dot_tn(edge_in[:, pl.ds(aligned(to * 384, 128), 384)], gbefore[...]).astype(BF16)
        w[j, 384:] = dot_tn(s.hidden[:, pl.ds(aligned(to * 128, 128), 128)], s.lin[...]).astype(BF16)

    edge_job = edge_weights_sum(links, edge_refs, RE, fill_edge, s.e_grad)
    next(edge_job)
    moved = s.moved
    moved[...] = dot_nt(gbefore[...], ef[D : 2 * D]).astype(BF16)
    back_out, back_in = s.back_out, s.back_in
    back_out[...] = to_slots(dot(s.send_hot_t[512:1024], moved[...]))
    back_wait = links.send_many(
        G, graph_peer, lambda m: back_out.at[m], back_in.at[g], back_in.at[pl.ds(0, G - 1)]
    )
    back_in[g] = back_out[g]
    next(edge_job)
    next(node_job)
    s.part_grads[...] = dot(s.send_hot_t[:512], moved[...])
    s.coarse_part[...] = dot(s.send_hot_t[1024:], moved[...])
    moved[...] = dot_nt(gbefore[...], ef[2 * D :]).astype(BF16)
    s.coarse_part[...] = s.coarse_part[...] + dot(s.recv_hot_t[N:], moved[...])
    coarse_grad = s.v_coarse_grad
    total = coarse_sum(links, s.coarse_part, s.a2_src, s.a2_rs, s.a2_z, s.a2_ag, coarse_grad)
    next(total)
    next(node_job)
    s.recv_own[...] = dot(s.recv_hot_t[:N], moved[...])
    s.v_edge_grad[...] = s.gnext[...] + dot_nt(gbefore[...], ef[:D])
    edge_out = links.local(s.v_edge_grad, s.edge_grad)
    extra = node_refs.extra
    first = dot_tn(node_in[N:, pl.ds(aligned(y * 256, 128), 256)], s.n_gbefore[N:])
    extra[0, :RN] = first[:RN]
    extra[1, : 256 - RN] = first[RN:]
    extra[1, 256 - RN : RN] = dot_tn(s.n_hidden[N:, pl.ds(aligned(y * 128, 128), 128)], s.n_lin[N:])
    extra[:, RN:] = jnp.zeros((NC, NZ * ZR - RN, D), F32)
    next(edge_job)
    next(node_job)
    next(total)

    back_wait()
    s.halo[...] = from_slots(back_in[...])
    s.part_grads[...] = s.part_grads[...] + dot(s.halo_hot_t[...], s.halo[...])
    p_y = s.p_y
    for j in range(4):
        p_y[j] = s.part_grads[pl.ds(aligned(xor4(y, j) * N, 16), N), :].astype(BF16)
    node_grad = s.v_node_grad
    part_job = halving(
        links, p_y, N // 2, s.p_a1, s.p_b1, s.p_a2, s.p_b2, lambda j: links.at(y=xor4(y, j)), node_grad
    )
    next(part_job)
    next(edge_job)
    next(node_job)
    next(total)
    next(part_job)
    next(node_job)
    next(edge_job)
    for _ in part_job:
        pass
    node_grad[...] = node_grad[...] + s.direct[:N] + s.recv_own[...]
    node_out = links.local(node_grad, s.node_grad)
    next(node_job)
    for _ in total:
        pass
    coarse_grad[...] = coarse_grad[...] + s.direct[N:]
    coarse_out = links.local(coarse_grad, s.coarse_grad)
    next(node_job)
    next(node_job)
    next(edge_job)
    for job in (node_job, edge_job):
        for _ in job:
            pass
    for copy in (edge_out, node_out, coarse_out):
        copy.wait()
    links.finish()


def finish(e_grad, n_grad, node_grad, coarse_grad, edge_grad, node_out, coarse_out, edge_out, ef, es, nf, ns, sems):
    copies = [
        pltpu.make_async_copy(src, dst, sems.at[k])
        for k, (src, dst) in enumerate(((edge_grad, edge_out), (coarse_grad, coarse_out), (node_grad, node_out)))
    ]
    for copy in copies:
        copy.start()
    for i in range(2 * RE // 16):
        row = i * 16
        core, block = row // RE, (row % RE) // 16
        out, at = (ef, row) if row < 384 else (es, row - 384)
        out[at : at + 16, :256] = e_grad[core, 2 * block].astype(F32)
        out[at : at + 16, 256:] = e_grad[core, 2 * block + 1].astype(F32)
    for i in range(2 * RN // ZR):
        row = i * ZR
        out, at = (nf, row) if row < 256 else (ns, row - 256)
        for j in range(NX):
            out[at : at + ZR, j * 128 : (j + 1) * 128] = n_grad[row // RN, j, (row % RN) // ZR].astype(F32)
    for copy in copies:
        copy.wait()


def program(
    node_lat, coarse_lat, edge_lat, senders, receivers, halo_rows, edge_live, edge_first, edge_second,
    node_first, node_second, edge_gain, node_gain, node_cotangent, coarse_cotangent, edge_cotangent,
):
    vmem = pl.BlockSpec(memory_space=pltpu.VMEM)
    anywhere = pl.BlockSpec(memory_space=pl.ANY)
    semaphores = [pltpu.SemaphoreType.DMA((count,)) for count in (SENDS, SENDS, LOCALS)]
    node_grad, coarse_grad, edge_grad, e_grad, n_grad = pl.pallas_call(
        body,
        out_shape=[jax.ShapeDtypeStruct(*v) for v in OUTPUTS.values()],
        in_specs=[vmem if small else anywhere for small in INPUTS.values()],
        out_specs=[anywhere] * len(OUTPUTS),
        scratch_shapes=[pltpu.VMEM(*v) for d in (SCRATCH, EDGE_JOB, NODE_JOB) for v in d.values()]
        + semaphores,
        compiler_params=pltpu.CompilerParams(
            collective_id=0, has_side_effects=True, vmem_limit_bytes=60 * 1024 * 1024
        ),
        name="layer",
    )(
        node_lat,
        coarse_lat,
        edge_lat,
        senders.reshape(1, E),
        receivers.reshape(1, E),
        halo_rows.T,
        edge_live.reshape(1, 1),
        edge_first,
        edge_second,
        node_first,
        node_second,
        edge_gain.reshape(1, D),
        node_gain.reshape(1, D),
        node_cotangent,
        coarse_cotangent,
        edge_cotangent,
    )
    shapes = [(N, D), (C, D), (E, D), (384, D), (128, D), (256, D), (128, D)]
    return pl.pallas_call(
        finish,
        out_shape=[jax.ShapeDtypeStruct(v, F32) for v in shapes],
        in_specs=[vmem, vmem, anywhere, anywhere, anywhere],
        out_specs=[anywhere] * 3 + [vmem] * 4,
        scratch_shapes=[pltpu.SemaphoreType.DMA((3,))],
        compiler_params=pltpu.CompilerParams(vmem_limit_bytes=60 * 1024 * 1024),
        name="finish",
    )(e_grad, n_grad, node_grad, coarse_grad, edge_grad)


def solution(mesh):
    rows = P(("graph", "feat"), None)
    return jax.shard_map(
        program,
        mesh=mesh,
        in_specs=(
            rows, P(), rows, P(("graph", "feat")), P(("graph", "feat")), rows, P(("graph", "feat")),
            P("feat", None), P("feat", None), P("feat", None), P("feat", None), P(), P(), rows, P(), rows,
        ),
        out_specs=(
            rows, P(), rows, P("feat", None), P("feat", None), P("feat", None), P("feat", None),
        ),
        check_vma=False,
    )
```

time: 626 us -> 163 us (0.26)
  waiting for transfers between devices: 367 us -> 0 us
  Pallas kernels: 0 us -> 162 us
  blocking collectives: 122 us -> 0 us
  local copies, waits for them, and re-layouts: 42.2 us -> 0 us
  other arithmetic: 37.1 us -> 0 us
  starting transfers between devices: 21.8 us -> 0 us
  matrix products: 19.5 us -> 0 us
  between operations: 15.1 us -> 1.29 us
    psum x1 -> x0, waiting for transfers between devices: 246 us -> none  [body(): lax.psum(coarse_partial, ('graph', 'feat'))]
    pallas_call x0 -> x2, Pallas kernels: none -> 162 us  [the longest x1 103 us: program(): pl.pallas_call(body, out_shape=[jax.ShapeDtypeStruct(*v) for v in OUTPUTS...]
    psum x1 -> x0, blocking collectives: 82.8 us -> none  [body(): coarse_total = lax.psum(coarse_aggregate, ('graph', 'feat'))]
    all_gather x3 -> x0, waiting for transfers between devices: 79.8 us -> none  [the longest x1 79.8 us: body(): summed = lax.all_gather(summed_piece, 'graph', axis=1, tiled=True)]
    all_gather x3 -> x0, blocking collectives: 38.8 us -> none  [the longest x1 14.1 us: body(): lax.all_gather(node_second, 'feat', axis=0, tiled=True)]
    all_to_all x2 -> x0, starting transfers between devices: 21.6 us -> none  [the longest x1 13.7 us: body(): lax.all_to_all(outgoing, 'graph', split_axis=0, concat_axis=0, tiled=True)]
    reduce_scatter x1 -> x0, waiting for transfers between devices: 20 us -> none  [body(): lax.psum_scatter(part_grads.astype(jnp.bfloat16), 'feat', scatter_dimensi...]
    all_to_all x2 -> x0, waiting for transfers between devices: 19.7 us -> none  [the longest x1 19.6 us: body(): lax.all_to_all(send_grads[part_rows:part_rows + slot_rows].astype(jnp.bfl...]
  transfers between devices with their start and end apart: 7 -> 0, of which waited for: 4 -> 0; matrix products, arithmetic and copies ran while one was open for 6% -> 0% of each run, Pallas kernels for 0% -> 0%
where the time goes in v1:
time: 163 us
  Pallas kernels  162 us (99%)
    pallas_call x1, Pallas kernels, program(): pl.pallas_call(body, out_shape=[jax.ShapeDtypeStruct(*v) for v in OUTPUTS...  103 us
    pallas_call x1, Pallas kernels, program(): pl.pallas_call(finish, out_shape=[jax.ShapeDtypeStruct(v, F32) for v in s...  59.1 us

profile of v1, /device:TPU:1, one launch (start us, length us, event | category | flops | bytes accessed | tf_op | source)
XLA Modules:
  0.0 163.3 jit_solution(2844343956978901232)
XLA Ops:
  1.3 102.8 %layer.1 = (f32[128,512]{1,0:T(8,128)}, f32[256,512]{1,0:T(8,128)}, f32[512,512]{1,0:T(8,128)}, bf16[2,32,16,256]{3,2,1,0:T(8,128)(2,1)}, bf16[2,4,8,32,128]{4,3,2,1,0:T(8,128)(2,1)}) custom-call(bf16[128,512]{1,0:T(8,128)(2,1)} %refs_0_.1, bf16[256,512]{1,0:T(8,128)(2,1)} %refs_1_.1, bf16[512,512]{1,0:T(8,128)(2,1)} %refs_2_.1, s32[1,512]{1,0:T(1,128)} %bitcast.8, ...), custom_call_target="tpu_custom_call" | custom-call | tf_op jit(solution)/shard_map/layer/pallas_call | solution.py:740
  104.1 59.1 %finish.1 = (f32[128,512]{1,0:T(8,128)}, f32[256,512]{1,0:T(8,128)}, f32[512,512]{1,0:T(8,128)}, f32[384,512]{1,0:T(8,128)}, f32[128,512]{1,0:T(8,128)}, /*index=5*/f32[256,512]{1,0:T(8,128)}, f32[128,512]{1,0:T(8,128)}) custom-call(bf16[2,32,16,256]{3,2,1,0:T(8,128)(2,1)} %get-tuple-element.12.e_grad, bf16[2,4,8,32,128]{4,3,2,1,0:T(8,128)(2,1)} %get-tuple-element.13.n_grad, ...), custom_call_target="tpu_custom_call" | custom-call | tf_op jit(solution)/shard_map/finish/pallas_call | solution.py:770

commit v2 on v1

--- a/solution.py
+++ b/solution.py
@@ -19,7 +19,7 @@
 NX, NY, NZ, NC = 4, 4, 8, 2
 G = NX * NZ * NC
 HALO = 8
-RE, RN = 256, 192
+RE, RN = 128, 192
 ZR = 32
 PLANE = NX * NZ
 
@@ -141,9 +141,9 @@
 
 EDGE_JOB, NODE_JOB = job_scratch(RE), job_scratch(RN)
 EDGE_JOB.update(
-    ps=((PLANE, 16, 256), BF16),
-    pr=((PLANE, 16, 256), BF16),
-    g=((PLANE, 16, 256), BF16),
+    ps=((PLANE, 16, 128), BF16),
+    pr=((PLANE, 16, 128), BF16),
+    g=((PLANE, 16, 128), BF16),
 )
 NODE_JOB.update(
     x=((NX, RN, 128), BF16),
@@ -156,7 +156,7 @@
     g=((NX, NZ, ZR, 128), BF16),
     extra=((NC, NZ * ZR, D), F32),
 )
-SENDS, LOCALS = 76, 16
+SENDS, LOCALS = 87, 17
 
 SMALL, LARGE = True, False
 INPUTS = dict(
@@ -168,7 +168,8 @@
     node_grad=((N, D), F32),
     coarse_grad=((C, D), F32),
     edge_grad=((E, D), F32),
-    e_grad=((NC, PLANE, 16, 256), BF16),
+    ea_grad=((NC, PLANE, 16, 128), BF16),
+    eb_grad=((NC, PLANE, 16, 128), BF16),
     n_grad=((NC, NX, NZ, ZR, 128), BF16),
 )
 
@@ -333,7 +334,7 @@
     yield from weight_scatter(links, t, r, fill)
     total, ps, pr, gathered = t.sum, t.ps, t.pr, t.g
     for i in range(PLANE):
-        ps[i] = total[(i // 2) * 16 : (i // 2) * 16 + 16, (i % 2) * 256 : (i % 2) * 256 + 256].astype(BF16)
+        ps[i] = total[(i // 4) * 16 : (i // 4) * 16 + 16, (i % 4) * 128 : (i % 4) * 128 + 128].astype(BF16)
     me = links.x * NZ + links.z
 
     def peer(k):
@@ -409,7 +410,8 @@
 def body(*refs):
     refs = iter(refs)
     s = Refs(zip([*INPUTS, *OUTPUTS, *SCRATCH], refs))
-    edge_refs, node_refs = Refs(zip(EDGE_JOB, refs)), Refs(zip(NODE_JOB, refs))
+    ea_refs, eb_refs = Refs(zip(EDGE_JOB, refs)), Refs(zip(EDGE_JOB, refs))
+    node_refs = Refs(zip(NODE_JOB, refs))
     links = Links(*refs)
     x, y, z, c, g = links.x, links.y, links.z, links.c, links.g
     y1, y2, y3 = xor4(y, 1), xor4(y, 2), xor4(y, 3)
@@ -633,13 +635,21 @@
     s.gbefore[...] = silu_backward(dot_nt(q, es[...]), before[...])
     gbefore = s.gbefore
 
-    def fill_edge(j, to):
-        w = edge_refs.w
-        w[j, :384] = dot_tn(edge_in[:, pl.ds(aligned(to * 384, 128), 384)], gbefore[...]).astype(BF16)
-        w[j, 384:] = dot_tn(s.hidden[:, pl.ds(aligned(to * 128, 128), 128)], s.lin[...]).astype(BF16)
-
-    edge_job = edge_weights_sum(links, edge_refs, RE, fill_edge, s.e_grad)
-    next(edge_job)
+    next(node_job)
+
+    def fill_ea(j, to):
+        ea_refs.w[j] = dot_tn(edge_in[:, pl.ds(aligned(to * 384, 128), 256)], gbefore[...]).astype(BF16)
+
+    def fill_eb(j, to):
+        first = dot_tn(edge_in[:, pl.ds(aligned(to * 384 + 256, 128), 128)], gbefore[...])
+        second = dot_tn(s.hidden[:, pl.ds(aligned(to * 128, 128), 128)], s.lin[...])
+        eb_refs.w[j, :128] = first.astype(BF16)
+        eb_refs.w[j, 128:] = second.astype(BF16)
+
+    ea_job = edge_weights_sum(links, ea_refs, RE, fill_ea, s.ea_grad)
+    eb_job = edge_weights_sum(links, eb_refs, RE, fill_eb, s.eb_grad)
+    next(ea_job)
+    next(eb_job)
     moved = s.moved
     moved[...] = dot_nt(gbefore[...], ef[D : 2 * D]).astype(BF16)
     back_out, back_in = s.back_out, s.back_in
@@ -648,7 +658,8 @@
         G, graph_peer, lambda m: back_out.at[m], back_in.at[g], back_in.at[pl.ds(0, G - 1)]
     )
     back_in[g] = back_out[g]
-    next(edge_job)
+    next(ea_job)
+    next(eb_job)
     next(node_job)
     s.part_grads[...] = dot(s.send_hot_t[:512], moved[...])
     s.coarse_part[...] = dot(s.send_hot_t[1024:], moved[...])
@@ -657,17 +668,22 @@
     coarse_grad = s.v_coarse_grad
     total = coarse_sum(links, s.coarse_part, s.a2_src, s.a2_rs, s.a2_z, s.a2_ag, coarse_grad)
     next(total)
-    next(node_job)
     s.recv_own[...] = dot(s.recv_hot_t[:N], moved[...])
     s.v_edge_grad[...] = s.gnext[...] + dot_nt(gbefore[...], ef[:D])
     edge_out = links.local(s.v_edge_grad, s.edge_grad)
+    next(ea_job)
+    next(node_job)
     extra = node_refs.extra
     first = dot_tn(node_in[N:, pl.ds(aligned(y * 256, 128), 256)], s.n_gbefore[N:])
     extra[0, :RN] = first[:RN]
     extra[1, : 256 - RN] = first[RN:]
     extra[1, 256 - RN : RN] = dot_tn(s.n_hidden[N:, pl.ds(aligned(y * 128, 128), 128)], s.n_lin[N:])
     extra[:, RN:] = jnp.zeros((NC, NZ * ZR - RN, D), F32)
-    next(edge_job)
+    next(eb_job)
+    next(total)
+    next(node_job)
+    next(ea_job)
+    next(eb_job)
     next(node_job)
     next(total)
 
@@ -682,25 +698,23 @@
         links, p_y, N // 2, s.p_a1, s.p_b1, s.p_a2, s.p_b2, lambda j: links.at(y=xor4(y, j)), node_grad
     )
     next(part_job)
-    next(edge_job)
-    next(node_job)
-    next(total)
+    next(ea_job)
+    next(node_job)
+    next(eb_job)
     next(part_job)
     next(node_job)
-    next(edge_job)
+    for _ in total:
+        pass
+    coarse_grad[...] = coarse_grad[...] + s.direct[N:]
+    coarse_out = links.local(coarse_grad, s.coarse_grad)
+    next(ea_job)
     for _ in part_job:
         pass
     node_grad[...] = node_grad[...] + s.direct[:N] + s.recv_own[...]
     node_out = links.local(node_grad, s.node_grad)
     next(node_job)
-    for _ in total:
-        pass
-    coarse_grad[...] = coarse_grad[...] + s.direct[N:]
-    coarse_out = links.local(coarse_grad, s.coarse_grad)
-    next(node_job)
-    next(node_job)
-    next(edge_job)
-    for job in (node_job, edge_job):
+    next(eb_job)
+    for job in (ea_job, node_job, eb_job):
         for _ in job:
             pass
     for copy in (edge_out, node_out, coarse_out):
@@ -708,19 +722,19 @@
     links.finish()
 
 
-def finish(e_grad, n_grad, node_grad, coarse_grad, edge_grad, node_out, coarse_out, edge_out, ef, es, nf, ns, sems):
+def finish(ea_grad, eb_grad, n_grad, node_grad, coarse_grad, edge_grad, node_out, coarse_out, edge_out, ef, es, nf, ns, sems):
     copies = [
         pltpu.make_async_copy(src, dst, sems.at[k])
         for k, (src, dst) in enumerate(((edge_grad, edge_out), (coarse_grad, coarse_out), (node_grad, node_out)))
     ]
     for copy in copies:
         copy.start()
-    for i in range(2 * RE // 16):
+    for i in range(4 * RE // 16):
         row = i * 16
-        core, block = row // RE, (row % RE) // 16
+        pieces, core, block = (ea_grad, eb_grad)[i // 16], (i // 8) % 2, i % 8
         out, at = (ef, row) if row < 384 else (es, row - 384)
-        out[at : at + 16, :256] = e_grad[core, 2 * block].astype(F32)
-        out[at : at + 16, 256:] = e_grad[core, 2 * block + 1].astype(F32)
+        for j in range(4):
+            out[at : at + 16, j * 128 : (j + 1) * 128] = pieces[core, 4 * block + j].astype(F32)
     for i in range(2 * RN // ZR):
         row = i * ZR
         out, at = (nf, row) if row < 256 else (ns, row - 256)
@@ -737,12 +751,12 @@
     vmem = pl.BlockSpec(memory_space=pltpu.VMEM)
     anywhere = pl.BlockSpec(memory_space=pl.ANY)
     semaphores = [pltpu.SemaphoreType.DMA((count,)) for count in (SENDS, SENDS, LOCALS)]
-    node_grad, coarse_grad, edge_grad, e_grad, n_grad = pl.pallas_call(
+    node_grad, coarse_grad, edge_grad, ea_grad, eb_grad, n_grad = pl.pallas_call(
         body,
         out_shape=[jax.ShapeDtypeStruct(*v) for v in OUTPUTS.values()],
         in_specs=[vmem if small else anywhere for small in INPUTS.values()],
         out_specs=[anywhere] * len(OUTPUTS),
-        scratch_shapes=[pltpu.VMEM(*v) for d in (SCRATCH, EDGE_JOB, NODE_JOB) for v in d.values()]
+        scratch_shapes=[pltpu.VMEM(*v) for d in (SCRATCH, EDGE_JOB, EDGE_JOB, NODE_JOB) for v in d.values()]
         + semaphores,
         compiler_params=pltpu.CompilerParams(
             collective_id=0, has_side_effects=True, vmem_limit_bytes=60 * 1024 * 1024
@@ -770,12 +784,12 @@
     return pl.pallas_call(
         finish,
         out_shape=[jax.ShapeDtypeStruct(v, F32) for v in shapes],
-        in_specs=[vmem, vmem, anywhere, anywhere, anywhere],
+        in_specs=[vmem] * 6,
         out_specs=[anywhere] * 3 + [vmem] * 4,
         scratch_shapes=[pltpu.SemaphoreType.DMA((3,))],
         compiler_params=pltpu.CompilerParams(vmem_limit_bytes=60 * 1024 * 1024),
         name="finish",
-    )(e_grad, n_grad, node_grad, coarse_grad, edge_grad)
+    )(ea_grad, eb_grad, n_grad, node_grad, coarse_grad, edge_grad)
 
 
 def solution(mesh):

time: 163 us -> 103 us (0.63)
  Pallas kernels: 162 us -> 102 us
    pallas_call x1, Pallas kernels: 59.1 us -> 4.26 us  [program(): pl.pallas_call(finish, out_shape=[jax.ShapeDtypeStruct(v, F32) for v in s...]
    pallas_call x1, Pallas kernels: 103 us -> 97.5 us  [program(): pl.pallas_call(body, out_shape=[jax.ShapeDtypeStruct(*v) for v in OUTPUTS...]
where the time goes in v2:
time: 103 us
  Pallas kernels  102 us (99%)
  between operations  1.29 us (1%)
    pallas_call x1, Pallas kernels, program(): pl.pallas_call(body, out_shape=[jax.ShapeDtypeStruct(*v) for v in OUTPUTS...  97.5 us
    pallas_call x1, Pallas kernels, program(): pl.pallas_call(finish, out_shape=[jax.ShapeDtypeStruct(v, F32) for v in s...  4.26 us

profile of v2, /device:TPU:1, one launch (start us, length us, event | category | flops | bytes accessed | tf_op | source)
XLA Modules:
  0.0 103.1 jit_solution(10492542459750215387)
XLA Ops:
  1.3 97.5 %layer.1 = (f32[128,512]{1,0:T(8,128)}, f32[256,512]{1,0:T(8,128)}, f32[512,512]{1,0:T(8,128)}, bf16[2,32,16,128]{3,2,1,0:T(8,128)(2,1)}, bf16[2,32,16,128]{3,2,...) custom-call(bf16[128,512]{1,0:T(8,128)(2,1)} %refs_0_.1, bf16[256,512]{1,0:T(8,128)(2,1)} %refs_1_.1, ...), custom_call_target="tpu_custom_call" | custom-call | tf_op jit(solution)/shard_map/layer/pallas_call | solution.py:754
  98.8 4.3 %finish.1 = (f32[128,512]{1,0:T(8,128)}, f32[256,512]{1,0:T(8,128)}, f32[512,512]{1,0:T(8,128)}, f32[384,512]{1,0:T(8,128)}, f32[128,512]{1,0:T(8,128)}, /*index=5*/f32[256,512]{1,0:T(8,128)}, f32[128,512]{1,0:T(8,128)}) custom-call(bf16[2,32,16,128]{3,2,1,0:T(8,128)(2,1)} %get-tuple-element.13.ea_grad, bf16[2,32,16,128]{3,2,1,0:T(8,128)(2,1)} %get-tuple-element.14.eb_grad, ...), custom_call_target="tpu_custom_call" | custom-call | tf_op jit(solution)/shard_map/finish/pallas_call | solution.py:784

commit v3 on v2

--- a/solution.py
+++ b/solution.py
@@ -83,6 +83,8 @@
     back_in=((G, 16, 256), BF16),
     halo=((G * HALO, D), BF16),
     edge_in=((E, 3 * D), BF16),
+    edge_in_t=((3 * D, E), BF16),
+    hidden_t=((D, E), BF16),
     before=((E, D), F32),
     hidden=((E, D), BF16),
     normed=((E, D), F32),
@@ -112,12 +114,14 @@
     a2_rs=((32, 16, 256), BF16),
     a2_z=((NZ, 16, 256), BF16),
     a2_ag=((32, 16, 256), BF16),
+    v_halo_rows=((HALO, G), jnp.int32),
+    v_senders=((1, E), jnp.int32),
+    v_receivers=((1, E), jnp.int32),
+    v_edge_gain=((1, D), F32),
+    v_node_gain=((1, D), F32),
     v_node_cot=((N, D), BF16),
     v_coarse_cot=((C, D), BF16),
     v_edge_cot=((E, D), BF16),
-    v_edge_grad=((E, D), F32),
-    v_node_grad=((N, D), F32),
-    v_coarse_grad=((C, D), F32),
     p_y=((NY, N, D), BF16),
     p_a1=((2, N // 2, D), BF16),
     p_b1=((2, N // 2, D), BF16),
@@ -147,22 +151,17 @@
 )
 NODE_JOB.update(
     x=((NX, RN, 128), BF16),
-    xa1=((2, RN // 2, 128), BF16),
-    xb1=((2, RN // 2, 128), BF16),
-    xa2=((RN // 2, 128), BF16),
-    xb2=((RN // 2, 128), BF16),
+    xr=((NX, RN, 128), BF16),
     zs=((NZ, ZR, 128), BF16),
     zr=((NZ, ZR, 128), BF16),
     g=((NX, NZ, ZR, 128), BF16),
     extra=((NC, NZ * ZR, D), F32),
 )
-SENDS, LOCALS = 87, 17
-
-SMALL, LARGE = True, False
-INPUTS = dict(
-    node_lat=LARGE, coarse_lat=LARGE, edge_lat=LARGE, senders=SMALL, receivers=SMALL, halo_rows=SMALL,
-    edge_live=SMALL, w_ef=LARGE, w_es=LARGE, w_nf=LARGE, w_ns=LARGE, edge_gain=SMALL, node_gain=SMALL,
-    node_cot=LARGE, coarse_cot=LARGE, edge_cot=LARGE,
+SENDS, LOCALS = 81, 17
+
+INPUTS = (
+    "node_lat", "coarse_lat", "edge_lat", "senders", "receivers", "halo_rows", "edge_live", "w_ef", "w_es",
+    "w_nf", "w_ns", "edge_gain", "node_gain", "node_cot", "coarse_cot", "edge_cot",
 )
 OUTPUTS = dict(
     node_grad=((N, D), F32),
@@ -352,20 +351,25 @@
     yield
     wait()
     copy = links.send(gathered, out.at[links.c], links.at(c=1 - links.c))
-    own = links.local(gathered, out.at[links.c])
+    out[links.c] = gathered[...]
     yield
     copy.wait_recv()
-    own.wait()
 
 
 def node_weights_sum(links, t, r, fill, out):
     yield from weight_scatter(links, t, r, fill)
-    for j in range(4):
-        t.x[j] = t.sum[:, pl.ds(aligned(xor4(links.x, j) * 128, 128), 128)].astype(BF16)
-    sub = t.sum.at[:, pl.ds(0, 128)]
-    yield from halving(
-        links, t.x, r // 2, t.xa1, t.xb1, t.xa2, t.xb2, lambda j: links.at(x=xor4(links.x, j)), sub
-    )
+    for j in range(NX):
+        t.x[j] = t.sum[:, j * 128 : (j + 1) * 128].astype(BF16)
+
+    def across(j):
+        to = (links.x + j) % NX
+        return to, links.at(x=to)
+
+    wait = links.send_many(NX, across, lambda m: t.x.at[m], t.xr.at[links.x], t.xr.at[pl.ds(0, NX - 1)])
+    t.xr[links.x] = t.x[links.x]
+    yield
+    wait()
+    sub = jnp.sum(t.xr[...].astype(F32), axis=0)
     blocks = r // ZR
     for i in range(NZ):
         t.zs[i] = sub[i * ZR : (i + 1) * ZR].astype(BF16) if i < blocks else jnp.zeros((ZR, 128), BF16)
@@ -386,25 +390,16 @@
     wait = links.send_many(NZ, along, lambda m: own.at[links.z], own.at[links.z], own.at[pl.ds(0, NZ - 1)])
     yield
     wait()
-    x1, x2, x3 = xor4(links.x, 1), xor4(links.x, 2), xor4(links.x, 3)
-    every, lo, hi = pl.ds(0, blocks), pl.ds(0, blocks // 2), pl.ds(blocks // 2, blocks // 2)
+    every = pl.ds(0, blocks)
     mine = t.g.at[links.x, every]
-    a = links.send(mine, mine, links.at(x=x1))
-    b = links.send(mine, mine, links.at(x=x3))
-    yield
-    a.wait_recv()
-    a = links.send(t.g.at[x1, lo], t.g.at[x1, lo], links.at(x=x3))
-    b.wait_recv()
-    b = links.send(t.g.at[x3, hi], t.g.at[x3, hi], links.at(x=x1))
-    yield
-    a.wait_recv()
-    b.wait_recv()
+    wait = links.send_many(NX, across, lambda m: mine, mine, t.g.at[pl.ds(0, NX - 1), every])
+    yield
+    wait()
     result = t.g.at[:, every]
     copy = links.send(result, out.at[links.c, :, every], links.at(c=1 - links.c))
-    local = links.local(result, out.at[links.c, :, every])
+    out[links.c] = t.g[...]
     yield
     copy.wait_recv()
-    local.wait()
 
 
 def body(*refs):
@@ -412,6 +407,7 @@
     s = Refs(zip([*INPUTS, *OUTPUTS, *SCRATCH], refs))
     ea_refs, eb_refs = Refs(zip(EDGE_JOB, refs)), Refs(zip(EDGE_JOB, refs))
     node_refs = Refs(zip(NODE_JOB, refs))
+    s.update(live=next(refs))
     links = Links(*refs)
     x, y, z, c, g = links.x, links.y, links.z, links.c, links.g
     y1, y2, y3 = xor4(y, 1), xor4(y, 2), xor4(y, 3)
@@ -434,6 +430,9 @@
 
     lax.fori_loop(1, G, greet_graph, 0)
     lax.fori_loop(0, 24, greet_plane, 0)
+    live_copy = links.local(s.edge_live, s.live)
+    codes_copies = [links.local(s[name], s["v_" + name]) for name in ("halo_rows", "senders", "receivers")]
+    gain_copies = [links.local(s[name], s["v_" + name]) for name in ("edge_gain", "node_gain")]
     early = [
         links.local(s.node_lat, nodes.at[y]),
         links.local(s.node_lat, node_in.at[pl.ds(0, N), pl.ds(0, D)]),
@@ -463,7 +462,9 @@
             hot_ref[:, j * 128 : (j + 1) * 128] = jnp.where(down == lanes + j * 128, 1.0, 0.0).astype(BF16)
             hot_t_ref[j * 128 : (j + 1) * 128, :] = jnp.where(across == subs + j * 128, 1.0, 0.0).astype(BF16)
 
-    codes = s.halo_rows[...]
+    for copy in codes_copies + gain_copies:
+        copy.wait()
+    codes = s.v_halo_rows[...]
     spread = (
         lax.broadcasted_iota(jnp.int32, (G, G * HALO), 0)
         == lax.broadcasted_iota(jnp.int32, (G, G * HALO), 1) // HALO
@@ -542,10 +543,11 @@
     )
     in_slots[g] = out_slots[g]
 
-    live = s.edge_live[...]
+    live_copy.wait()
+    live = s.live[0]
     alive_row = lax.broadcasted_iota(jnp.int32, (1, E), 1) < live
-    hot(jnp.where(alive_row, s.senders[...], -1), s.send_hot, s.send_hot_t, 1280)
-    hot(jnp.where(alive_row, s.receivers[...], -1), s.recv_hot, s.recv_hot_t, N + C)
+    hot(jnp.where(alive_row, s.v_senders[...], -1), s.send_hot, s.send_hot_t, 1280)
+    hot(jnp.where(alive_row, s.v_receivers[...], -1), s.recv_hot, s.recv_hot_t, N + C)
     node_lat, coarse_lat = node_in[:N, :D], node_in[N:, :D]
     edge_in[:, 2 * D :] = (
         dot(s.recv_hot[:, :N], node_lat) + dot(s.recv_hot[:, N:], coarse_lat)
@@ -561,7 +563,6 @@
     before = s.before
     before[...] = dot(edge_in[:, :D], ef[:D]) + dot(edge_in[:, 2 * D :], ef[2 * D :])
 
-    node_forward, node_swap = weight_step2(node_weights)
 
     halo_wait()
     s.halo[...] = from_slots(in_slots[...])
@@ -569,11 +570,12 @@
         edge_in[:, D : 2 * D].astype(F32) + dot(s.send_hot[:, 512:1024], s.halo[...])
     ).astype(BF16)
     before[...] = before[...] + dot(edge_in[:, D : 2 * D], ef[D : 2 * D])
+    node_forward, node_swap = weight_step2(node_weights)
     s.hidden[...] = (before[...] * jax.nn.sigmoid(before[...])).astype(BF16)
     normed, inverse = normalise(dot(s.hidden[...], es[...]))
     s.normed[...] = normed
     s.inverse[...] = inverse
-    edge_next = (edge_in[:, :D].astype(F32) + normed * s.edge_gain[...]).astype(BF16)
+    edge_next = (edge_in[:, :D].astype(F32) + normed * s.v_edge_gain[...]).astype(BF16)
     s.coarse_part[...] = dot(s.recv_hot_t[N:], edge_next)
     total = coarse_sum(
         links, s.coarse_part, s.a1_src, s.a1_rs, s.a1_z, s.a1_ag, s.coarse_total
@@ -598,11 +600,10 @@
 
     def node_pass_backward(rows):
         up = node_up(rows)
-        q = norm_backward(up, s.node_gain[...], s.n_normed[rows], s.n_inverse[rows])
+        q = norm_backward(up, s.v_node_gain[...], s.n_normed[rows], s.n_inverse[rows])
         zz = silu_backward(dot_nt(q, ns[...]), s.n_before[rows])
         s.n_lin[rows] = q
         s.n_gbefore[rows] = zz
-        s.direct[rows] = up + dot_nt(zz, nf[:D])
         s.gagg[rows] = dot_nt(zz, nf[D:]).astype(BF16)
 
     own, coarse = slice(0, N), slice(N, N + C)
@@ -621,6 +622,8 @@
     next(node_job)
     next(total)
     next(node_job)
+    s.edge_in_t[...] = jnp.transpose(edge_in[...])
+    s.hidden_t[...] = jnp.transpose(s.hidden[...])
     for _ in total:
         pass
     node_in[N:, D:] = s.coarse_total[...]
@@ -630,7 +633,7 @@
     s.gnext[...] = s.v_edge_cot[...].astype(F32) + dot(s.recv_hot[...], s.gagg[...])
     alive = lax.broadcasted_iota(jnp.int32, (E, 1), 0) < live
     upstream = jnp.where(alive, s.gnext[...], 0.0)
-    q = norm_backward(upstream, s.edge_gain[...], s.normed[...], s.inverse[...])
+    q = norm_backward(upstream, s.v_edge_gain[...], s.normed[...], s.inverse[...])
     s.lin[...] = q
     s.gbefore[...] = silu_backward(dot_nt(q, es[...]), before[...])
     gbefore = s.gbefore
@@ -638,11 +641,11 @@
     next(node_job)
 
     def fill_ea(j, to):
-        ea_refs.w[j] = dot_tn(edge_in[:, pl.ds(aligned(to * 384, 128), 256)], gbefore[...]).astype(BF16)
+        ea_refs.w[j] = dot(s.edge_in_t[pl.ds(aligned(to * 384, 128), 256), :], gbefore[...]).astype(BF16)
 
     def fill_eb(j, to):
-        first = dot_tn(edge_in[:, pl.ds(aligned(to * 384 + 256, 128), 128)], gbefore[...])
-        second = dot_tn(s.hidden[:, pl.ds(aligned(to * 128, 128), 128)], s.lin[...])
+        first = dot(s.edge_in_t[pl.ds(aligned(to * 384 + 256, 128), 128), :], gbefore[...])
+        second = dot(s.hidden_t[pl.ds(aligned(to * 128, 128), 128), :], s.lin[...])
         eb_refs.w[j, :128] = first.astype(BF16)
         eb_refs.w[j, 128:] = second.astype(BF16)
 
@@ -665,27 +668,24 @@
     s.coarse_part[...] = dot(s.send_hot_t[1024:], moved[...])
     moved[...] = dot_nt(gbefore[...], ef[2 * D :]).astype(BF16)
     s.coarse_part[...] = s.coarse_part[...] + dot(s.recv_hot_t[N:], moved[...])
-    coarse_grad = s.v_coarse_grad
-    total = coarse_sum(links, s.coarse_part, s.a2_src, s.a2_rs, s.a2_z, s.a2_ag, coarse_grad)
-    next(total)
     s.recv_own[...] = dot(s.recv_hot_t[:N], moved[...])
-    s.v_edge_grad[...] = s.gnext[...] + dot_nt(gbefore[...], ef[:D])
-    edge_out = links.local(s.v_edge_grad, s.edge_grad)
-    next(ea_job)
-    next(node_job)
+    s.edge_grad[...] = s.gnext[...] + dot_nt(gbefore[...], ef[:D])
+    s.direct[:N] = s.v_node_cot[...].astype(F32) + dot_nt(s.n_gbefore[:N], nf[:D])
+    s.direct[N:] = s.v_coarse_cot[...].astype(F32) + dot_nt(s.n_gbefore[N:], nf[:D])
     extra = node_refs.extra
     first = dot_tn(node_in[N:, pl.ds(aligned(y * 256, 128), 256)], s.n_gbefore[N:])
     extra[0, :RN] = first[:RN]
     extra[1, : 256 - RN] = first[RN:]
     extra[1, 256 - RN : RN] = dot_tn(s.n_hidden[N:, pl.ds(aligned(y * 128, 128), 128)], s.n_lin[N:])
     extra[:, RN:] = jnp.zeros((NC, NZ * ZR - RN, D), F32)
+    next(ea_job)
+    next(node_job)
     next(eb_job)
+    coarse_grad = s.coarse_grad
+    total = coarse_sum(links, s.coarse_part, s.a2_src, s.a2_rs, s.a2_z, s.a2_ag, coarse_grad)
     next(total)
-    next(node_job)
     next(ea_job)
     next(eb_job)
-    next(node_job)
-    next(total)
 
     back_wait()
     s.halo[...] = from_slots(back_in[...])
@@ -693,54 +693,59 @@
     p_y = s.p_y
     for j in range(4):
         p_y[j] = s.part_grads[pl.ds(aligned(xor4(y, j) * N, 16), N), :].astype(BF16)
-    node_grad = s.v_node_grad
+    node_grad = s.node_grad
     part_job = halving(
         links, p_y, N // 2, s.p_a1, s.p_b1, s.p_a2, s.p_b2, lambda j: links.at(y=xor4(y, j)), node_grad
     )
     next(part_job)
+    next(total)
+    next(node_job)
     next(ea_job)
+    next(total)
+    next(part_job)
     next(node_job)
     next(eb_job)
-    next(part_job)
-    next(node_job)
+    for _ in part_job:
+        pass
+    node_grad[...] = node_grad[...] + s.direct[:N] + s.recv_own[...]
     for _ in total:
         pass
     coarse_grad[...] = coarse_grad[...] + s.direct[N:]
-    coarse_out = links.local(coarse_grad, s.coarse_grad)
     next(ea_job)
-    for _ in part_job:
-        pass
-    node_grad[...] = node_grad[...] + s.direct[:N] + s.recv_own[...]
-    node_out = links.local(node_grad, s.node_grad)
     next(node_job)
     next(eb_job)
     for job in (ea_job, node_job, eb_job):
         for _ in job:
             pass
-    for copy in (edge_out, node_out, coarse_out):
-        copy.wait()
     links.finish()
 
 
-def finish(ea_grad, eb_grad, n_grad, node_grad, coarse_grad, edge_grad, node_out, coarse_out, edge_out, ef, es, nf, ns, sems):
-    copies = [
+def finish(*refs):
+    sources, results, held, sems = refs[:6], refs[6:13], refs[13:17], refs[17]
+    ea_grad, eb_grad, n_grad = sources[3:]
+    ef, es, nf, ns = held
+    stores = [
         pltpu.make_async_copy(src, dst, sems.at[k])
-        for k, (src, dst) in enumerate(((edge_grad, edge_out), (coarse_grad, coarse_out), (node_grad, node_out)))
+        for k, (src, dst) in enumerate(zip((*sources[:3], *held), results))
     ]
-    for copy in copies:
-        copy.start()
+    for k in range(3):
+        stores[k].start()
     for i in range(4 * RE // 16):
         row = i * 16
         pieces, core, block = (ea_grad, eb_grad)[i // 16], (i // 8) % 2, i % 8
         out, at = (ef, row) if row < 384 else (es, row - 384)
         for j in range(4):
             out[at : at + 16, j * 128 : (j + 1) * 128] = pieces[core, 4 * block + j].astype(F32)
+    stores[3].start()
+    stores[4].start()
     for i in range(2 * RN // ZR):
         row = i * ZR
         out, at = (nf, row) if row < 256 else (ns, row - 256)
         for j in range(NX):
             out[at : at + ZR, j * 128 : (j + 1) * 128] = n_grad[row // RN, j, (row % RN) // ZR].astype(F32)
-    for copy in copies:
+    stores[5].start()
+    stores[6].start()
+    for copy in stores:
         copy.wait()
 
 
@@ -748,16 +753,15 @@
     node_lat, coarse_lat, edge_lat, senders, receivers, halo_rows, edge_live, edge_first, edge_second,
     node_first, node_second, edge_gain, node_gain, node_cotangent, coarse_cotangent, edge_cotangent,
 ):
-    vmem = pl.BlockSpec(memory_space=pltpu.VMEM)
-    anywhere = pl.BlockSpec(memory_space=pl.ANY)
+    vmem, anywhere = pl.BlockSpec(memory_space=pltpu.VMEM), pl.BlockSpec(memory_space=pl.ANY)
     semaphores = [pltpu.SemaphoreType.DMA((count,)) for count in (SENDS, SENDS, LOCALS)]
-    node_grad, coarse_grad, edge_grad, ea_grad, eb_grad, n_grad = pl.pallas_call(
+    results = pl.pallas_call(
         body,
-        out_shape=[jax.ShapeDtypeStruct(*v) for v in OUTPUTS.values()],
-        in_specs=[vmem if small else anywhere for small in INPUTS.values()],
-        out_specs=[anywhere] * len(OUTPUTS),
+        out_shape=[pltpu.VMEM(*v) for v in OUTPUTS.values()],
+        in_specs=[anywhere] * len(INPUTS),
+        out_specs=[vmem] * len(OUTPUTS),
         scratch_shapes=[pltpu.VMEM(*v) for d in (SCRATCH, EDGE_JOB, EDGE_JOB, NODE_JOB) for v in d.values()]
-        + semaphores,
+        + [pltpu.SMEM((1,), jnp.int32)] + semaphores,
         compiler_params=pltpu.CompilerParams(
             collective_id=0, has_side_effects=True, vmem_limit_bytes=60 * 1024 * 1024
         ),
@@ -769,7 +773,7 @@
         senders.reshape(1, E),
         receivers.reshape(1, E),
         halo_rows.T,
-        edge_live.reshape(1, 1),
+        edge_live,
         edge_first,
         edge_second,
         node_first,
@@ -785,11 +789,11 @@
         finish,
         out_shape=[jax.ShapeDtypeStruct(v, F32) for v in shapes],
         in_specs=[vmem] * 6,
-        out_specs=[anywhere] * 3 + [vmem] * 4,
-        scratch_shapes=[pltpu.SemaphoreType.DMA((3,))],
+        out_specs=[anywhere] * 7,
+        scratch_shapes=[pltpu.VMEM(v, F32) for v in shapes[3:]] + [pltpu.SemaphoreType.DMA((7,))],
         compiler_params=pltpu.CompilerParams(vmem_limit_bytes=60 * 1024 * 1024),
         name="finish",
-    )(ea_grad, eb_grad, n_grad, node_grad, coarse_grad, edge_grad)
+    )(*(pltpu.with_memory_space_constraint(v, pltpu.VMEM) for v in results))
 
 
 def solution(mesh):

time: 103 us -> 99.5 us (0.966)
  Pallas kernels: 102 us -> 98.1 us
    pallas_call x1, Pallas kernels: 4.26 us -> 1.89 us  [program(): pl.pallas_call(finish, out_shape=[jax.ShapeDtypeStruct(v, F32) for v in s...]
    pallas_call x1, Pallas kernels: 97.5 us -> 96.2 us  [program(): pl.pallas_call(body, out_shape=[pltpu.VMEM(*v) for v in OUTPUTS.values()]...]
where the time goes in v3:
time: 99.5 us; the launch traced here: 99.4 us
  Pallas kernels  98.1 us (99%)
  between operations  1.29 us (1%)
    pallas_call x1, Pallas kernels, program(): pl.pallas_call(body, out_shape=[pltpu.VMEM(*v) for v in OUTPUTS.values()]...  96.2 us

profile of v3, /device:TPU:1, one launch (start us, length us, event | category | flops | bytes accessed | tf_op | source)
XLA Modules:
  0.0 99.4 jit_solution(2551527942070933166)
XLA Ops:
  1.3 96.2 %layer.1 = (f32[128,512]{1,0:T(8,128)S(1)}, f32[256,512]{1,0:T(8,128)S(1)}, f32[512,512]{1,0:T(8,128)S(1)}, bf16[2,32,16,128]{3,2,1,0:T(8,128)(2,1)S(1)}, bf16[2...) custom-call(bf16[128,512]{1,0:T(8,128)(2,1)} %refs_0_.1, bf16[256,512]{1,0:T(8,128)(2,1)} %refs_1_.1, ...), custom_call_target="tpu_custom_call" | custom-call | tf_op jit(solution)/shard_map/layer/pallas_call | solution.py:758
  97.5 1.9 %finish.1 = (f32[128,512]{1,0:T(8,128)}, f32[256,512]{1,0:T(8,128)}, f32[512,512]{1,0:T(8,128)}, f32[384,512]{1,0:T(8,128)}, f32[128,512]{1,0:T(8,128)}, /*index=5*/f32[256,512]{1,0:T(8,128)}, f32[128,512]{1,0:T(8,128)}) custom-call(f32[128,512]{1,0:T(8,128)S(1)} %get-tuple-element.13.refs_0_, f32[256,512]{1,0:T(8,128)S(1)} %get-tuple-element.14.refs_1_, ...), custom_call_target="tpu_custom_call" | custom-call | tf_op jit(solution)/shard_map/finish/pallas_call | solution.py:788

commit v4 on v3

--- a/solution.py
+++ b/solution.py
@@ -60,9 +60,9 @@
     return grad.astype(BF16)
 
 
-def silu_backward(grad_hidden, before):
+def silu_slope(before):
     sigma = jax.nn.sigmoid(before)
-    return (grad_hidden * sigma * (1.0 + before * (1.0 - sigma))).astype(BF16)
+    return sigma * (1.0 + before * (1.0 - sigma))
 
 
 SCRATCH = dict(
@@ -110,10 +110,15 @@
     a1_rs=((32, 16, 256), BF16),
     a1_z=((NZ, 16, 256), BF16),
     a1_ag=((32, 16, 256), BF16),
-    a2_src=((32, 16, 256), BF16),
-    a2_rs=((32, 16, 256), BF16),
+    a2_out=((C // 2, D), BF16),
+    a2_in=((C // 2, D), BF16),
+    a2_src=((16, 16, 256), BF16),
+    a2_rs=((16, 16, 256), BF16),
     a2_z=((NZ, 16, 256), BF16),
-    a2_ag=((32, 16, 256), BF16),
+    a2_ag=((16, 16, 256), BF16),
+    a2_back=((16, 16, 256), BF16),
+    coarse_base=((C, D), F32),
+    slope=((E, D), F32),
     v_halo_rows=((HALO, G), jnp.int32),
     v_senders=((1, E), jnp.int32),
     v_receivers=((1, E), jnp.int32),
@@ -145,8 +150,10 @@
 
 EDGE_JOB, NODE_JOB = job_scratch(RE), job_scratch(RN)
 EDGE_JOB.update(
-    ps=((PLANE, 16, 128), BF16),
-    pr=((PLANE, 16, 128), BF16),
+    x=((NX, RE, 128), BF16),
+    xr=((NX, RE, 128), BF16),
+    zs=((NZ, 16, 128), BF16),
+    zr=((NZ, 16, 128), BF16),
     g=((PLANE, 16, 128), BF16),
 )
 NODE_JOB.update(
@@ -157,7 +164,7 @@
     g=((NX, NZ, ZR, 128), BF16),
     extra=((NC, NZ * ZR, D), F32),
 )
-SENDS, LOCALS = 81, 17
+SENDS, LOCALS = 85, 17
 
 INPUTS = (
     "node_lat", "coarse_lat", "edge_lat", "senders", "receivers", "halo_rows", "edge_live", "w_ef", "w_es",
@@ -219,7 +226,7 @@
     def send_many(self, count, peer, src, dst, whole):
         k = self.slot()
 
-        def body(j, carry):
+        for j in range(1, count):
             index, device = peer(j)
             pltpu.make_async_remote_copy(
                 src_ref=src(index),
@@ -229,9 +236,6 @@
                 device_id=device,
                 device_id_type=MESH,
             ).start()
-            return carry
-
-        lax.fori_loop(1, count, body, 0)
         self.sent.append(("many", whole, k))
 
         def wait():
@@ -283,8 +287,9 @@
     me = (links.x * 4 + links.y) * 2 + links.c
 
     def peer(j):
-        m = (me + j * 11) % 32
-        return m, links.at(x=m // 8, y=(m // 2) % 4, c=m % 2)
+        dx, dy, dc = (j * 11 % 32) // 8, (j * 11 % 8) // 2, j % 2
+        px, py, pc = lax.rem(links.x + dx, NX), lax.rem(links.y + dy, NY), 1 - links.c if dc else links.c
+        return (px * 4 + py) * 2 + pc, links.at(x=px, y=py, c=pc)
 
     for i in range(32):
         src[i] = source[(i // 2) * 16 : (i // 2) * 16 + 16, (i % 2) * 256 : (i % 2) * 256 + 256].astype(BF16)
@@ -295,7 +300,7 @@
     zb[links.z] = jnp.sum(rs[...].astype(F32), axis=0).astype(BF16)
 
     def along(j):
-        to = (links.z + j * 3) % 8
+        to = lax.rem(links.z + j * 3 % NZ, NZ)
         return to, links.at(z=to)
 
     wait = links.send_many(8, along, lambda m: zb.at[links.z], zb.at[links.z], zb.at[pl.ds(0, 7)])
@@ -307,6 +312,53 @@
     wait()
     for i in range(32):
         out[(i // 2) * 16 : (i // 2) * 16 + 16, (i % 2) * 256 : (i % 2) * 256 + 256] = ag[i].astype(out.dtype)
+
+
+def coarse_sum_by_chip(links, s, out):
+    half = C // 2
+    mine, theirs = aligned(links.c * half, 16), aligned((1 - links.c) * half, 16)
+    other = links.at(c=1 - links.c)
+    s.a2_out[...] = s.coarse_part[pl.ds(theirs, half), :].astype(BF16)
+    copy = links.send(s.a2_out, s.a2_in, other)
+    yield
+    copy.wait_recv()
+    source = s.coarse_part[pl.ds(mine, half), :] + s.a2_in[...].astype(F32)
+    me = links.x * NY + links.y
+
+    def peer(j):
+        px, py = lax.rem(links.x + (j * 7 % 16) // 4, NX), lax.rem(links.y + j * 7 % 4, NY)
+        return px * NY + py, links.at(x=px, y=py)
+
+    for i in range(16):
+        s.a2_src[i] = source[(i // 2) * 16 : (i // 2) * 16 + 16, (i % 2) * 256 : (i % 2) * 256 + 256].astype(BF16)
+    wait = links.send_many(16, peer, lambda m: s.a2_src.at[m], s.a2_rs.at[me], s.a2_rs.at[pl.ds(0, 15)])
+    s.a2_rs[me] = s.a2_src[me]
+    yield
+    wait()
+    zb = s.a2_z
+    zb[links.z] = jnp.sum(s.a2_rs[...].astype(F32), axis=0).astype(BF16)
+
+    def along(j):
+        to = lax.rem(links.z + j * 3 % NZ, NZ)
+        return to, links.at(z=to)
+
+    wait = links.send_many(NZ, along, lambda m: zb.at[links.z], zb.at[links.z], zb.at[pl.ds(0, NZ - 1)])
+    yield
+    wait()
+    ag = s.a2_ag
+    ag[me] = jnp.sum(zb[...].astype(F32), axis=0).astype(BF16)
+    wait = links.send_many(16, peer, lambda m: ag.at[me], ag.at[me], ag.at[pl.ds(0, 15)])
+    yield
+    wait()
+    copy = links.send(ag, s.a2_back, other)
+    for i in range(16):
+        rows = pl.ds(aligned(mine + (i // 2) * 16, 16), 16)
+        out[rows, (i % 2) * 256 : (i % 2) * 256 + 256] = ag[i].astype(out.dtype)
+    yield
+    copy.wait_recv()
+    for i in range(16):
+        rows = pl.ds(aligned(theirs + (i // 2) * 16, 16), 16)
+        out[rows, (i % 2) * 256 : (i % 2) * 256 + 256] = s.a2_back[i].astype(out.dtype)
 
 
 def weight_scatter(links, t, r, fill):
@@ -331,20 +383,34 @@
 
 def edge_weights_sum(links, t, r, fill, out):
     yield from weight_scatter(links, t, r, fill)
-    total, ps, pr, gathered = t.sum, t.ps, t.pr, t.g
-    for i in range(PLANE):
-        ps[i] = total[(i // 4) * 16 : (i // 4) * 16 + 16, (i % 4) * 128 : (i % 4) * 128 + 128].astype(BF16)
+    for j in range(NX):
+        t.x[j] = t.sum[:, j * 128 : (j + 1) * 128].astype(BF16)
+
+    def across(j):
+        to = lax.rem(links.x + j, NX)
+        return to, links.at(x=to)
+
+    def along(j):
+        to = lax.rem(links.z + j * 3 % NZ, NZ)
+        return to, links.at(z=to)
+
+    wait = links.send_many(NX, across, lambda m: t.x.at[m], t.xr.at[links.x], t.xr.at[pl.ds(0, NX - 1)])
+    t.xr[links.x] = t.x[links.x]
+    yield
+    wait()
+    t.zs[...] = jnp.sum(t.xr[...].astype(F32), axis=0).astype(BF16).reshape(NZ, 16, 128)
+    wait = links.send_many(NZ, along, lambda m: t.zs.at[m], t.zr.at[links.z], t.zr.at[pl.ds(0, NZ - 1)])
+    t.zr[links.z] = t.zs[links.z]
+    yield
+    wait()
+    gathered = t.g
     me = links.x * NZ + links.z
 
     def peer(k):
-        m = (me + k * 11) % PLANE
-        return m, links.at(x=m // NZ, z=m % NZ)
-
-    wait = links.send_many(PLANE, peer, lambda m: ps.at[m], pr.at[me], pr.at[pl.ds(0, PLANE - 1)])
-    pr[me] = ps[me]
-    yield
-    wait()
-    gathered[me] = jnp.sum(pr[...].astype(F32), axis=0).astype(BF16)
+        px, pz = lax.rem(links.x + (k * 11 % 32) // 8, NX), lax.rem(links.z + k * 11 % 8, NZ)
+        return px * NZ + pz, links.at(x=px, z=pz)
+
+    gathered[me] = jnp.sum(t.zr[...].astype(F32), axis=0).astype(BF16)
     wait = links.send_many(
         PLANE, peer, lambda m: gathered.at[me], gathered.at[me], gathered.at[pl.ds(0, PLANE - 1)]
     )
@@ -362,7 +428,7 @@
         t.x[j] = t.sum[:, j * 128 : (j + 1) * 128].astype(BF16)
 
     def across(j):
-        to = (links.x + j) % NX
+        to = lax.rem(links.x + j, NX)
         return to, links.at(x=to)
 
     wait = links.send_many(NX, across, lambda m: t.x.at[m], t.xr.at[links.x], t.xr.at[pl.ds(0, NX - 1)])
@@ -375,7 +441,7 @@
         t.zs[i] = sub[i * ZR : (i + 1) * ZR].astype(BF16) if i < blocks else jnp.zeros((ZR, 128), BF16)
 
     def along(j):
-        to = (links.z + j * 3) % NZ
+        to = lax.rem(links.z + j * 3 % NZ, NZ)
         return to, links.at(z=to)
 
     wait = links.send_many(NZ, along, lambda m: t.zs.at[m], t.zr.at[links.z], t.zr.at[pl.ds(0, NZ - 1)])
@@ -418,18 +484,13 @@
 
     barrier = pltpu.get_barrier_semaphore()
 
-    def greet_graph(j, carry):
+    for j in range(1, G):
         pl.semaphore_signal(barrier, inc=1, device_id=((g + j) % G, y), device_id_type=MESH)
-        return carry
-
-    def greet_plane(j, carry):
-        k = j // 3
-        device = links.at(x=k // 2, c=k % 2, y=(y + 1 + j % 3) % 4)
-        pl.semaphore_signal(barrier, inc=1, device_id=device, device_id_type=MESH)
-        return carry
-
-    lax.fori_loop(1, G, greet_graph, 0)
-    lax.fori_loop(0, 24, greet_plane, 0)
+    for k in range(NX * NC):
+        for there in (y1, y2, y3):
+            pl.semaphore_signal(
+                barrier, inc=1, device_id=links.at(x=k // 2, c=k % 2, y=there), device_id_type=MESH
+            )
     live_copy = links.local(s.edge_live, s.live)
     codes_copies = [links.local(s[name], s["v_" + name]) for name in ("halo_rows", "senders", "receivers")]
     gain_copies = [links.local(s[name], s["v_" + name]) for name in ("edge_gain", "node_gain")]
@@ -526,16 +587,18 @@
             swap.append(links.send(src, src, other))
         return swap
 
+    edge_weights = weight_step1(("ef", "es"))
     for copy in (a_hi, b_lo, a2, b2):
         copy.wait_recv()
-    edge_weights = weight_step1(("ef", "es"))
 
     out_slots, in_slots = s.out_slots, s.in_slots
     part_nodes = nodes[...].reshape(NY * N, D)
     out_slots[...] = to_slots(dot(s.halo_hot[...], part_nodes))
 
     def graph_peer(j):
-        to = (g + j * 29) % G
+        q, odd, r = (j - 1) // 16, (j - 1) % 2, (((j - 1) % 16) // 2 + 1) % 8
+        dx, dz, dc = r // 2, (4 - q + odd * (1 + 2 * q)) % NZ, r % 2
+        to = (lax.rem(x + dx, NX) * NZ + lax.rem(z + dz, NZ)) * NC + (1 - c if dc else c)
         return to, (to, y)
 
     halo_wait = links.send_many(
@@ -590,7 +653,10 @@
         return s[name][...].astype(F32)
 
     def node_pass_forward(rows):
-        a = dot(node_in[rows], nf[...])
+        if rows.start == 0:
+            a = dot(node_in[rows], nf[...])
+        else:
+            a = s.coarse_base[...] + dot(node_in[rows, D:], nf[D:])
         hidden = (a * jax.nn.sigmoid(a)).astype(BF16)
         s.n_before[rows] = a
         s.n_hidden[rows] = hidden
@@ -601,7 +667,7 @@
     def node_pass_backward(rows):
         up = node_up(rows)
         q = norm_backward(up, s.v_node_gain[...], s.n_normed[rows], s.n_inverse[rows])
-        zz = silu_backward(dot_nt(q, ns[...]), s.n_before[rows])
+        zz = (dot_nt(q, ns[...]) * silu_slope(s.n_before[rows])).astype(BF16)
         s.n_lin[rows] = q
         s.n_gbefore[rows] = zz
         s.gagg[rows] = dot_nt(zz, nf[D:]).astype(BF16)
@@ -622,6 +688,8 @@
     next(node_job)
     next(total)
     next(node_job)
+    s.slope[...] = silu_slope(before[...])
+    s.coarse_base[...] = dot(node_in[N:, :D], nf[:D])
     s.edge_in_t[...] = jnp.transpose(edge_in[...])
     s.hidden_t[...] = jnp.transpose(s.hidden[...])
     for _ in total:
@@ -635,10 +703,9 @@
     upstream = jnp.where(alive, s.gnext[...], 0.0)
     q = norm_backward(upstream, s.v_edge_gain[...], s.normed[...], s.inverse[...])
     s.lin[...] = q
-    s.gbefore[...] = silu_backward(dot_nt(q, es[...]), before[...])
+    s.gbefore[...] = (dot_nt(q, es[...]) * s.slope[...]).astype(BF16)
     gbefore = s.gbefore
 
-    next(node_job)
 
     def fill_ea(j, to):
         ea_refs.w[j] = dot(s.edge_in_t[pl.ds(aligned(to * 384, 128), 256), :], gbefore[...]).astype(BF16)
@@ -652,6 +719,7 @@
     ea_job = edge_weights_sum(links, ea_refs, RE, fill_ea, s.ea_grad)
     eb_job = edge_weights_sum(links, eb_refs, RE, fill_eb, s.eb_grad)
     next(ea_job)
+    next(node_job)
     next(eb_job)
     moved = s.moved
     moved[...] = dot_nt(gbefore[...], ef[D : 2 * D]).astype(BF16)
@@ -663,11 +731,13 @@
     back_in[g] = back_out[g]
     next(ea_job)
     next(eb_job)
-    next(node_job)
     s.part_grads[...] = dot(s.send_hot_t[:512], moved[...])
     s.coarse_part[...] = dot(s.send_hot_t[1024:], moved[...])
     moved[...] = dot_nt(gbefore[...], ef[2 * D :]).astype(BF16)
     s.coarse_part[...] = s.coarse_part[...] + dot(s.recv_hot_t[N:], moved[...])
+    coarse_grad = s.coarse_grad
+    total = coarse_sum_by_chip(links, s, coarse_grad)
+    next(total)
     s.recv_own[...] = dot(s.recv_hot_t[:N], moved[...])
     s.edge_grad[...] = s.gnext[...] + dot_nt(gbefore[...], ef[:D])
     s.direct[:N] = s.v_node_cot[...].astype(F32) + dot_nt(s.n_gbefore[:N], nf[:D])
@@ -678,14 +748,14 @@
     extra[1, : 256 - RN] = first[RN:]
     extra[1, 256 - RN : RN] = dot_tn(s.n_hidden[N:, pl.ds(aligned(y * 128, 128), 128)], s.n_lin[N:])
     extra[:, RN:] = jnp.zeros((NC, NZ * ZR - RN, D), F32)
+    next(node_job)
+    next(ea_job)
+    next(eb_job)
+    next(total)
     next(ea_job)
     next(node_job)
     next(eb_job)
-    coarse_grad = s.coarse_grad
-    total = coarse_sum(links, s.coarse_part, s.a2_src, s.a2_rs, s.a2_z, s.a2_ag, coarse_grad)
-    next(total)
     next(ea_job)
-    next(eb_job)
 
     back_wait()
     s.halo[...] = from_slots(back_in[...])
@@ -698,22 +768,24 @@
         links, p_y, N // 2, s.p_a1, s.p_b1, s.p_a2, s.p_b2, lambda j: links.at(y=xor4(y, j)), node_grad
     )
     next(part_job)
+    next(node_job)
     next(total)
-    next(node_job)
+    next(eb_job)
     next(ea_job)
+    next(part_job)
     next(total)
-    next(part_job)
     next(node_job)
     next(eb_job)
     for _ in part_job:
         pass
     node_grad[...] = node_grad[...] + s.direct[:N] + s.recv_own[...]
+    next(ea_job)
+    next(total)
+    next(node_job)
+    next(eb_job)
     for _ in total:
         pass
     coarse_grad[...] = coarse_grad[...] + s.direct[N:]
-    next(ea_job)
-    next(node_job)
-    next(eb_job)
     for job in (ea_job, node_job, eb_job):
         for _ in job:
             pass
@@ -734,8 +806,8 @@
         row = i * 16
         pieces, core, block = (ea_grad, eb_grad)[i // 16], (i // 8) % 2, i % 8
         out, at = (ef, row) if row < 384 else (es, row - 384)
-        for j in range(4):
-            out[at : at + 16, j * 128 : (j + 1) * 128] = pieces[core, 4 * block + j].astype(F32)
+        for j in range(NX):
+            out[at : at + 16, j * 128 : (j + 1) * 128] = pieces[core, j * NZ + block].astype(F32)
     stores[3].start()
     stores[4].start()
     for i in range(2 * RN // ZR):

time: 99.5 us -> 94.9 us (0.954)
  Pallas kernels: 98.1 us -> 93.4 us
    pallas_call x1, Pallas kernels: 96.2 us -> 91.5 us  [program(): pl.pallas_call(body, out_shape=[pltpu.VMEM(*v) for v in OUTPUTS.values()]...]
where the time goes in v4:
time: 94.9 us; the launch traced here: 94.8 us
  Pallas kernels  93.4 us (98%)
  between operations  1.45 us (2%)
    pallas_call x1, Pallas kernels, program(): pl.pallas_call(body, out_shape=[pltpu.VMEM(*v) for v in OUTPUTS.values()]...  91.5 us

profile of v4, /device:TPU:1, one launch (start us, length us, event | category | flops | bytes accessed | tf_op | source)
XLA Modules:
  0.0 94.8 jit_solution(11865314792193342237)
XLA Ops:
  1.3 91.5 %layer.1 = (f32[128,512]{1,0:T(8,128)S(1)}, f32[256,512]{1,0:T(8,128)S(1)}, f32[512,512]{1,0:T(8,128)S(1)}, bf16[2,32,16,128]{3,2,1,0:T(8,128)(2,1)S(1)}, bf16[2...) custom-call(bf16[128,512]{1,0:T(8,128)(2,1)} %refs_0_.1, bf16[256,512]{1,0:T(8,128)(2,1)} %refs_1_.1, ...), custom_call_target="tpu_custom_call" | custom-call | tf_op jit(solution)/shard_map/layer/pallas_call | solution.py:830
  92.8 1.9 %finish.1 = (f32[128,512]{1,0:T(8,128)}, f32[256,512]{1,0:T(8,128)}, f32[512,512]{1,0:T(8,128)}, f32[384,512]{1,0:T(8,128)}, f32[128,512]{1,0:T(8,128)}, /*index=5*/f32[256,512]{1,0:T(8,128)}, f32[128,512]{1,0:T(8,128)}) custom-call(f32[128,512]{1,0:T(8,128)S(1)} %get-tuple-element.13.refs_0_, f32[256,512]{1,0:T(8,128)S(1)} %get-tuple-element.14.refs_1_, ...), custom_call_target="tpu_custom_call" | custom-call | tf_op jit(solution)/shard_map/finish/pallas_call | solution.py:860
